TPU v7x, 256 devices: a whole 4x4x8 slice. The times are simulated.
256 devices in a mesh: prompt: 4 (over x), prefix: 8 (over y, core), sample: 8 (over z).
Axes of the slice: x: 4, y: 4, z: 8, core: 2. Of those that a mesh axis runs over, the one named last changes fastest.
Arguments:
- new_hidden: bfloat16 [16, 16, 4, 5120], P('prompt', 'prefix'), may hold values from -6 to 6
- query_projection_weight: bfloat16 [5120, 8192], P(('prompt', 'prefix'), 'sample'), may hold values from -0.078125 to 0.078125
- key_projection_weight: bfloat16 [5120, 1024], P(('prompt', 'prefix'), 'sample'), may hold values from -0.078125 to 0.078125
- value_projection_weight: bfloat16 [5120, 1024], P(('prompt', 'prefix'), 'sample'), may hold values from -0.078125 to 0.078125
- w_out: bfloat16 [8192, 5120], P('sample', ('prompt', 'prefix')), may hold values from -0.0625 to 0.0625
- query_norm_gain: bfloat16 [128], replicated, may hold values from 0.5 to 2
- key_norm_gain: bfloat16 [128], replicated, may hold values from 2 to 8
- prefix_keys: bfloat16 [16, 32768, 8, 128], P('prompt', 'prefix', 'sample'), may hold values from -170 to 170
- prompt_cache_values: bfloat16 [16, 32768, 8, 128], P('prompt', 'prefix', 'sample'), may hold values from -6 to 6
- generated_keys: bfloat16 [16, 16, 512, 8, 128], P('prompt', 'prefix', None, 'sample'), may hold values from -6 to 6
- generated_values: bfloat16 [16, 16, 512, 8, 128], P('prompt', 'prefix', None, 'sample'), may hold values from -6 to 6
- prompt_lengths: int32 [16], P('prompt'), may hold values from 8192 to 32768, as said below
- window_lengths: int32 [16, 16], P('prompt', 'prefix'), may hold values from 1 to 512, as said below
Outputs:
- block_out: bfloat16 [16, 16, 4, 5120], P('prompt', 'prefix', None, 'sample')
Inputs may be any that keep to these rules, and one draw needn't show every extreme that they name: `prompt_lengths`: the longest prompt has exactly 32768 tokens. `window_lengths`: some sample's window holds exactly 512 tokens.
All inputs are finite; a program needn't handle non-finite values.
Results may differ from a plain program's by a relative error of at most 0.027.
Values may be sent and summed in bfloat16 or wider, within the bound.
A program may use at most 128 MiB of HBM per device.

v0:
```python
import math

import jax
import jax.numpy as jnp
from jax import lax
from jax.sharding import PartitionSpec as P


def apply_norm(raw, gain):
    scale = lax.rsqrt(jnp.mean(raw * raw, axis=-1, keepdims=True) + 1e-06)
    return raw * scale * gain.astype(jnp.float32)


def on_device(
    new_hidden,
    query_projection_weight,
    key_projection_weight,
    value_projection_weight,
    w_out,
    query_norm_gain,
    key_norm_gain,
    prefix_keys,
    prompt_cache_values,
    generated_keys,
    generated_values,
    prompt_lengths,
    window_lengths,
):
    prompt_list, samples_here, decode_step_count, model_width = new_hidden.shape
    head_dim = query_norm_gain.shape[0]
    heads_here = query_projection_weight.shape[1] // head_dim
    kv_here = key_projection_weight.shape[1] // head_dim
    query_group_width = heads_here // kv_here
    rows_here = prompt_list * samples_here * decode_step_count
    token_matrix = new_hidden.reshape(rows_here, model_width)
    weights = jnp.concatenate(
        (query_projection_weight, key_projection_weight, value_projection_weight), axis=1
    )
    spread = lax.all_to_all(
        token_matrix, ("prompt", "prefix"), split_axis=1, concat_axis=0, tiled=True
    )
    projected = lax.psum_scatter(
        jnp.dot(spread, weights, preferred_element_type=jnp.float32),
        ("prompt", "prefix"),
        scatter_dimension=0,
        tiled=True,
    )
    query_cols = heads_here * head_dim
    key_cols = kv_here * head_dim
    query_vector = apply_norm(
        projected[:, :query_cols].reshape(
            prompt_list, samples_here, decode_step_count, kv_here, query_group_width, head_dim
        ),
        query_norm_gain,
    ).astype(jnp.bfloat16)
    fresh_key = apply_norm(
        projected[:, query_cols : query_cols + key_cols].reshape(
            prompt_list, samples_here, decode_step_count, kv_here, head_dim
        ),
        key_norm_gain,
    ).astype(jnp.bfloat16)
    fresh_value = (
        projected[:, query_cols + key_cols :]
        .reshape(prompt_list, samples_here, decode_step_count, kv_here, head_dim)
        .astype(jnp.bfloat16)
    )
    scale = 1.0 / math.sqrt(head_dim)
    all_queries = lax.all_gather(query_vector, "prefix", axis=1, tiled=True)
    prefix_len = prefix_keys.shape[1]
    offset = lax.axis_index("prefix") * prefix_len
    positions = offset + jnp.arange(prefix_len)
    valid = positions[None, :] < prompt_lengths[:, None]
    pre_mask = valid[:, None, None, None, None, :]
    scores = (
        jnp.einsum(
            "psrhgd,pnhd->psrhgn", all_queries, prefix_keys, preferred_element_type=jnp.float32
        )
        * scale
    )
    scores = jnp.where(pre_mask, scores, -1e30)
    local_top = jnp.max(scores, axis=-1)
    weight = jnp.where(pre_mask, jnp.exp(scores - local_top[..., None]), 0.0)
    local_total = jnp.sum(weight, axis=-1)
    local_numer = jnp.einsum(
        "psrhgn,pnhd->psrhgd",
        weight.astype(jnp.bfloat16),
        prompt_cache_values,
        preferred_element_type=jnp.float32,
    )
    own_start = lax.axis_index("prefix") * samples_here
    global_top = lax.pmax(local_top, "prefix")
    factor = jnp.exp(local_top - global_top)
    numer, total = (
        lax.psum_scatter(
            (local_numer * factor[..., None]).astype(jnp.bfloat16),
            "prefix",
            scatter_dimension=1,
            tiled=True,
        ).astype(jnp.float32),
        lax.psum_scatter(
            (local_total * factor).astype(jnp.bfloat16), "prefix", scatter_dimension=1, tiled=True
        ).astype(jnp.float32),
    )
    top = lax.dynamic_slice_in_dim(global_top, own_start, samples_here, 1)
    win_len = generated_keys.shape[2]
    win_mask = (jnp.arange(win_len)[None, None, :] < window_lengths[:, :, None])[
        :, :, None, None, None, :
    ]
    win_scores = (
        jnp.einsum(
            "psrhgd,pswhd->psrhgw", query_vector, generated_keys, preferred_element_type=jnp.float32
        )
        * scale
    )
    win_scores = jnp.where(win_mask, win_scores, -1e30)
    causal = jnp.arange(decode_step_count)[None, :] <= jnp.arange(decode_step_count)[:, None]
    own_mask = causal[None, None, :, None, None, :]
    own_scores = (
        jnp.einsum(
            "psrhgd,psthd->psrhgt", query_vector, fresh_key, preferred_element_type=jnp.float32
        )
        * scale
    )
    own_scores = jnp.where(own_mask, own_scores, -1e30)
    final_top = jnp.maximum(
        top, jnp.maximum(jnp.max(win_scores, axis=-1), jnp.max(own_scores, axis=-1))
    )
    win_weight = jnp.where(win_mask, jnp.exp(win_scores - final_top[..., None]), 0.0)
    own_weight = jnp.where(own_mask, jnp.exp(own_scores - final_top[..., None]), 0.0)
    carried = jnp.exp(top - final_top)
    total = total * carried + jnp.sum(win_weight, axis=-1) + jnp.sum(own_weight, axis=-1)
    numer = numer * carried[..., None]
    numer = numer + jnp.einsum(
        "psrhgw,pswhd->psrhgd",
        win_weight.astype(jnp.bfloat16),
        generated_values,
        preferred_element_type=jnp.float32,
    )
    numer = numer + jnp.einsum(
        "psrhgt,psthd->psrhgd",
        own_weight.astype(jnp.bfloat16),
        fresh_value,
        preferred_element_type=jnp.float32,
    )
    attended = (
        (numer / total[..., None]).astype(jnp.bfloat16).reshape(rows_here, heads_here * head_dim)
    )
    stacked = jnp.dot(
        lax.all_gather(attended, ("prompt", "prefix"), axis=0, tiled=True),
        w_out,
        preferred_element_type=jnp.float32,
    )
    returned = lax.all_to_all(
        stacked.astype(jnp.bfloat16), ("prompt", "prefix"), split_axis=0, concat_axis=1, tiled=True
    ).astype(stacked.dtype)
    summed = lax.psum_scatter(
        returned.astype(jnp.bfloat16), "sample", scatter_dimension=1, tiled=True
    )
    return summed.reshape(prompt_list, samples_here, decode_step_count, -1)


def solution(mesh):
    return jax.shard_map(
        on_device,
        mesh=mesh,
        in_specs=(
            P("prompt", "prefix", None, None),
            P(("prompt", "prefix"), "sample"),
            P(("prompt", "prefix"), "sample"),
            P(("prompt", "prefix"), "sample"),
            P("sample", ("prompt", "prefix")),
            P(),
            P(),
            P("prompt", "prefix", "sample", None),
            P("prompt", "prefix", "sample", None),
            P("prompt", "prefix", None, "sample", None),
            P("prompt", "prefix", None, "sample", None),
            P("prompt"),
            P("prompt", "prefix"),
        ),
        out_specs=P("prompt", "prefix", None, "sample"),
        check_vma=False,
    )
```

profile of v0, /device:TPU:32, one launch (start us, length us, event | category | flops | bytes accessed | tf_op | source)
XLA Modules:
  0.0 397.8 jit_solution(17628036072473061999)
XLA Ops:
  6.5 1.7 all_to_all.28
  8.3 0.3 copy.27
  8.6 18.3 %all_to_all.38 = bf16[32,32,160]{2,0,1:T(8,128)(2,1)S(1)} all-to-all(bf16[32,32,160]{2,0,1:T(8,128)(2,1)S(1)} %copy.27), channel_id=1, replica_groups=mesh['prompt'=4,'prefix'=8,'sample'=8] {'prompt','prefix'}, dimensions={1} | all-to-all | bytes 655360 | tf_op jit(solution)/shard_map/all_to_all | solution.py:39
  26.9 4.3 %convolution_bitcast_fusion = f32[1024,1280]{0,1:T(8,128)} fusion(bf16[1024,160]{1,0:T(8,128)(2,1)S(1)} %bitcast.235, bf16[160,128]{1,0:T(8,128)(2,1)} %param.16, bf16[160,128]{1,0:T(8,128)(2,1)} %param.15, bf16[160,1024]{1,0:T(8,128)(2,1)} %param.14), kind=kOutput, calls=%fused_computation.10 | convolution fusion | flops 420659200 | bytes 5980160 | tf_op jit(solution)/shard_map/dot_general | solution.py:43
  31.1 5.9 %copy.41 = f32[1024,1280]{1,0:T(8,128)} copy(f32[1024,1280]{0,1:T(8,128)} %convolution_bitcast_fusion) | data formatting | bytes 10485760
  37.1 0.7 convert_element_type.66
  37.8 0.7 convert_element_type.73
  38.5 0.8 copy.29
  39.2 1.3 dynamic-slice
  41.3 0.7 broadcast_compare_fusion
  42.0 86.8 %reduce-scatter.11.cloned.1.call-done = f32[32,1280]{1,0:T(8,128)} async-done(((f32[1024,1280]{1,0:T(8,128)}), f32[32,1280]{1,0:T(8,128)}) %reduce-scatter.11.cloned.1.call-update) | async-done | bytes 163856 | tf_op jit(solution)/shard_map/reduce_scatter | solution.py:42
  128.8 0.9 slice_bitcast_fusion
  130.0 13.1 %all_gather.6 = bf16[4,16,4,1,8,128]{5,4,2,1,0,3:T(8,128)(2,1)S(1)} all-gather(bf16[4,2,4,1,8,128]{5,4,2,1,0,3:T(8,128)(2,1)S(1)} %multiply_convert_fusion.1), channel_id=1, replica_groups=mesh['prompt'=4,'prefix'=8,'sample'=8] {'prefix'}, dimensions={1}, use_global_device_ids=true | all-gather | bytes 589824 | tf_op jit(solution)/shard_map/all_gather | solution.py:68
  143.1 15.7 %fusion.1 = (f32[4,16,4,8]{3,2,1,0:T(4,128)S(1)}, f32[4,16,4,8,4096]{4,3,2,1,0:T(8,128)}) fusion(pred[4,4096]{1,0:T(4,128)(4,1)S(1)} %broadcast_compare_fusion, bf16[4,4096,1,128]{3,1,2,0:T(8,128)(2,1)} %param.20, bf16[4,16,4,1,8,128]{5,4,2,1,0,3:T(8,128)(2,1)S(1)} %all_gather.6), kind=kOutput, calls=%fused_computation.3 | convolution fusion | flops 2172647424 | bytes 38297600 | tf_op jit(solution)/shard_map/psrhgd,pnhd->psrhgn/dot_general | solution.py:75
  158.8 27.0 %pmax.7 = f32[4,16,4,1,8]{4,2,1,0,3:T(4,128)S(1)} all-reduce(f32[4,16,4,1,8]{4,2,1,0,3:T(4,128)S(1)} %bitcast.234), channel_id=1, replica_groups=mesh['prompt'=4,'prefix'=8,'sample'=8] {'prefix'}, use_global_device_ids=true, to_apply=%region_3.4 | all-reduce | flops 2048 | bytes 16384 | tf_op jit(solution)/shard_map/pmax | solution.py:91
  185.8 0.8 multiply_reduce_fusion.1
  186.8 15.6 %fusion.2 = f32[4,16,4,8]{3,2,1,0:T(4,128)S(1)} fusion(f32[4,16,4,8,4096]{4,3,2,1,0:T(8,128)} %get-tuple-element.12, f32[4,16,4,8]{3,2,1,0:T(4,128)S(1)} %get-tuple-element.11, pred[4,4096]{1,0:T(4,128)(4,1)S(1)} %broadcast_compare_fusion), kind=kLoop, calls=%fused_computation.4 | loop fusion | flops 41940992 | bytes 33587200 | tf_op jit(solution)/shard_map/reduce_sum | solution.py:83
  202.4 15.9 %fusion.28 = bf16[4,16,4,1,8,128]{5,4,2,1,0,3:T(8,128)(2,1)} fusion(bf16[4,4096,1,128]{3,1,2,0:T(8,128)(2,1)} %param.21, f32[4,16,4,8,4096]{4,3,2,1,0:T(8,128)} %get-tuple-element.12, f32[4,16,4,8]{3,2,1,0:T(4,128)S(1)} %get-tuple-element.11, pred[4,4096]{1,0:T(4,128)(4,1)S(1)} %broadcast_compare_fusion, f32[4,16,4,8]{3,2,1,0:T(4,128)S(1)} %get-tuple-element.8), kind=kOutput, calls=%fused_computation.19 | convolution fusion | flops 2189950976 | bytes 38305792 | tf_op jit(solution)/shard_map/psrhgn,pnhd->psrhgd/dot_general | solution.py:84
  218.6 0.6 fusion.77
  219.2 0.5 fusion.78
  219.9 0.7 slice.19
  221.1 23.9 %all-reduce.1 = bf16[4,16,4,1,8]{4,2,1,0,3:T(4,128)(2,1)S(1)} all-reduce(bf16[4,16,4,1,8]{4,2,1,0,3:T(4,128)(2,1)S(1)} %get-tuple-element.7), channel_id=4, replica_groups=mesh['prompt'=4,'prefix'=8,'sample'=8] {'prefix'}, use_global_device_ids=true, to_apply=%region_9.10.clone | all-reduce | flops 2048 | bytes 8192
  245.1 36.7 %all-reduce.4.cloned.1.call-done = bf16[4,16,4,1,8,128]{5,4,2,1,0,3:T(8,128)(2,1)} async-done(((bf16[4,16,4,1,8,128]{5,4,2,1,0,3:T(8,128)(2,1)}), bf16[4,16,4,1,8,128]{5,4,2,1,0,3:T(8,128)(2,1)}) %all-reduce.4.cloned.1.call-update) | async-done | bytes 524304
  281.7 1.2 fusion.38
  282.9 0.6 copy.56
  283.6 48.8 %all-gather.2.cloned.1.call-done = bf16[1024,1024]{1,0:T(8,128)(2,1)} async-done(((bf16[32,1024]{1,0:T(8,128)(2,1)}), bf16[1024,1024]{1,0:T(8,128)(2,1)}) %all-gather.2.cloned.1.call-update) | async-done | bytes 2097168 | tf_op jit(solution)/shard_map/all_gather | solution.py:149
  332.4 2.4 convolution_convert_fusion
  335.1 16.1 %all_to_all.39 = bf16[32,32,160]{2,1,0:T(8,128)(2,1)S(1)} all-to-all(bf16[32,32,160]{2,1,0:T(8,128)(2,1)S(1)} %bitcast.237), channel_id=1, replica_groups=mesh['prompt'=4,'prefix'=8,'sample'=8] {'prompt','prefix'}, dimensions={0} | all-to-all | bytes 655360 | tf_op jit(solution)/shard_map/all_to_all | solution.py:153
  351.1 1.4 copy.49
  352.6 37.0 %reduce-scatter.13.cloned.1.call-done = bf16[640,32]{1,0:T(8,128)(2,1)} async-done(((bf16[5120,32]{1,0:T(8,128)(2,1)}), bf16[640,32]{1,0:T(8,128)(2,1)}) %reduce-scatter.13.cloned.1.call-update) | async-done | bytes 40976
  389.6 1.0 copy.48
  390.6 0.6 reshape.247
  (30 shorter events, 1.9 us)
Async XLA Ops:
  6.5 212.0 %copy-start = (bf16[4,2,512,1,128]{4,2,3,1,0:T(8,128)(2,1)S(1)}, bf16[4,2,512,1,128]{4,2,3,1,0:T(8,128)(2,1)}, u32[]{:S(2)}) copy-start(bf16[4,2,512,1,128]{4,2,3,1,0:T(8,128)(2,1)} %param.22) | copy-start | bytes 3145732
  6.5 122.2 %reduce-scatter.11.cloned.1.call-start = ((), (), s32[]{:S(2)}) async-start(), calls=%async_computation.5 | async-start | bytes 5406720 | tf_op jit(solution)/shard_map/reduce_scatter | solution.py:42
  37.1 244.7 %all-reduce.4.cloned.1.call-start = ((), (), s32[]{:S(2)}) async-start(), calls=%async_computation.7 | async-start | bytes 1048576
  202.4 79.3 %copy-start.1 = (bf16[4,2,512,1,128]{4,2,3,1,0:T(8,128)(2,1)S(1)}, bf16[4,2,512,1,128]{4,2,3,1,0:T(8,128)(2,1)}, u32[]{:S(2)}) copy-start(bf16[4,2,512,1,128]{4,2,3,1,0:T(8,128)(2,1)} %param.23) | copy-start | bytes 3145732
  202.4 130.0 %copy-start.2 = (bf16[1024,160]{0,1:T(8,128)(2,1)S(1)}, bf16[1024,160]{0,1:T(8,128)(2,1)}, u32[]{:S(2)}) copy-start(bf16[1024,160]{0,1:T(8,128)(2,1)} %param.17) | copy-start | bytes 983044
  218.3 114.1 %all-gather.2.cloned.1.call-start = ((), (), s32[]{:S(2)}) async-start(), calls=%async_computation.4 | async-start | bytes 2162688 | tf_op jit(solution)/shard_map/all_gather | solution.py:149
  283.6 106.0 %reduce-scatter.13.cloned.1.call-start = ((), (), s32[]{:S(2)}) async-start(), calls=%async_computation.6 | async-start | bytes 1474560
Sparse Core Ops, SparseCore 0:
  37.2 91.5 reduce-scatter.10
  218.5 63.2 all-reduce.3
  284.3 48.0 all-gather.1
  352.7 36.8 reduce-scatter.12
where the time goes:
time: 400 us; the launch traced here: 398 us
  waiting for transfers between devices  209 us (52%)
  blocking collectives  98.4 us (25%)
  matrix products  40.8 us (10%)
  other arithmetic  19.3 us (5%)
  local copies, waits for them, and re-layouts  15.6 us (4%)
  between operations  14 us (4%)
    reduce_scatter x1, waiting for transfers between devices, on_device(): lax.psum_scatter(jnp.dot(spread, weights, preferred_element_type=jnp.floa...  86.8 us
    unnamed x6, waiting for transfers between devices  73.8 us
    all_gather x1, waiting for transfers between devices, on_device(): lax.all_gather(attended, ('prompt', 'prefix'), axis=0, tiled=True)  48.8 us
    pmax x1, blocking collectives, on_device(): global_top = lax.pmax(local_top, 'prefix')  27 us
    unnamed x1, blocking collectives  23.9 us
    all_to_all x1, blocking collectives, on_device(): lax.all_to_all(token_matrix, ('prompt', 'prefix'), split_axis=1, concat_a...  18.3 us
    all_to_all x1, blocking collectives, on_device(): lax.all_to_all(stacked.astype(jnp.bfloat16), ('prompt', 'prefix'), split_...  16.1 us
    dot_general x1, matrix products, on_device(): jnp.einsum('psrhgn,pnhd->psrhgd', weight.astype(jnp.bfloat16), prompt_cac...  15.9 us
  transfers between devices with their start and end apart: 4, of which 4 were waited for; matrix products, arithmetic and copies ran while one was open for 2% of the time, Pallas kernels for 0%

commit v1 on v0

v1 whole, which is shorter than its diff:
```python
import functools
import math

import jax
import jax.numpy as jnp
from jax import lax
from jax.experimental import pallas as pl
from jax.experimental.pallas import tpu as pltpu
from jax.sharding import PartitionSpec as P

MESH = pl.DeviceIdType.MESH
LOG2E = 1.4426950408889634
NT = (((1,), (1,)), ((), ()))


class Sends:
    def __init__(self, sems):
        self.sems = sems
        self.started = []

    def go(self, src, dst, recv, device):
        copy = pltpu.make_async_remote_copy(
            src_ref=src,
            dst_ref=dst,
            send_sem=self.sems.at[len(self.started)],
            recv_sem=recv,
            device_id=device,
            device_id_type=MESH,
        )
        copy.start()
        self.started.append(copy)

    def finish(self):
        for copy in self.started:
            copy.wait_send()


def arrived(ref, sem):
    pltpu.make_async_copy(ref, ref, sem).wait()


def greet(devices):
    barrier = pltpu.get_barrier_semaphore()
    for device in devices:
        pl.semaphore_signal(barrier, inc=1, device_id=device, device_id_type=MESH)
    pl.semaphore_wait(barrier, len(devices))


def norm(raw, gain):
    scale = lax.rsqrt(jnp.mean(raw * raw, axis=-1, keepdims=True) + 1e-06)
    return raw * scale * gain


def project_kernel(
    px, ny, batch,
    hid, wq, wk, wv, wo, qg, kg,
    q_out, k_out, v_out, wo_out,
    wbuf, tok, acc, part, red, qf, qscr,
    send, loc, w_sem, tw_sem, t_sem, r_sem, q_sem, o_sem, ot_sem,
):
    nn = 2 * ny
    x = lax.axis_index("prompt")
    n = lax.axis_index("prefix")
    y, c = lax.div(n, 2), lax.rem(n, 2)
    right, left = lax.rem(x + 1, px), lax.rem(x + px - 1, px)
    across = lax.rem(x + 2, px)
    rows = hid.shape[0]
    depth = wq.shape[0]
    qcols, kcols = wq.shape[1], wk.shape[1]
    pair = 2 * depth
    window = wbuf.shape[1]
    pad = window - pair
    to_right, to_left = {"prompt": right}, {"prompt": left}
    twin = {"prefix": 2 * y + 1 - c}
    peers = [lax.rem(y + i, ny) for i in range(1, ny)]
    others = [{"prefix": 2 * peer + c} for peer in peers]

    zero = jnp.zeros((px, pad, wbuf.shape[2]), wbuf.dtype)
    wbuf[:, 0:pad, :] = zero
    wbuf[:, pair : pair + pad, :] = zero

    greet([to_right, to_left, twin] + others)
    out = Sends(send)

    base = pl.multiple_of(pad * lax.rem(y, 2) + depth * c, 16)
    mine = pl.ds(base, depth)
    half = depth // 2
    first = pl.ds(base, half)
    second = pl.ds(pl.multiple_of(base + half, 16), half)
    base_t = pl.multiple_of(pad * lax.rem(y, 2) + depth * (1 - c), 16)
    theirs = pl.ds(base_t, depth)
    pieces = ((wq, 0, qcols), (wk, qcols, kcols), (wv, qcols + kcols, kcols))
    for piece, lo, width in pieces:
        spot = wbuf.at[x, mine, lo : lo + width]
        out.go(piece, spot, w_sem.at[0], to_right)
        out.go(piece, spot, w_sem.at[1], to_left)

    def start_of(block, chip):
        return pl.multiple_of(128 * lax.div(pair * ny * block + pair * chip, 128), 128)

    for peer, device in zip(peers, others):
        for block in range(px):
            out.go(
                hid.at[:, pl.ds(start_of(block, peer), window)],
                tok.at[y, block],
                t_sem.at[y],
                device,
            )
    for piece, lo, width in pieces:
        spot = wbuf.at[x, mine, lo : lo + width]
        out.go(piece, spot, tw_sem.at[0], twin)
    for piece, lo, width in pieces:
        spot = wbuf.at[x, mine, lo : lo + width]
        pltpu.make_async_copy(piece, spot, loc.at[0]).start()
    for block in range(px):
        pltpu.make_async_copy(
            hid.at[:, pl.ds(start_of(block, y), window)], tok.at[y, block], loc.at[1]
        ).start()

    orow = pl.ds(pl.multiple_of(depth * c, 16), depth)
    orow_t = pl.ds(pl.multiple_of(depth * (1 - c), 16), depth)
    ofirst = pl.ds(pl.multiple_of(depth * c, 16), half)
    osecond = pl.ds(pl.multiple_of(depth * c + half, 16), half)

    def multiply(block, start):
        lhs = tok[:, block].reshape(ny * rows, window)
        value = jnp.dot(lhs, wbuf[block], preferred_element_type=jnp.float32)
        if start:
            acc[...] = value
        else:
            acc[...] += value

    arrived(wbuf.at[x, mine], loc.at[0])
    arrived(tok.at[y], loc.at[1])
    for peer in peers:
        arrived(tok.at[peer], t_sem.at[peer])
    arrived(wbuf.at[x, theirs], tw_sem.at[0])
    multiply(x, True)

    arrived(wbuf.at[left, mine], w_sem.at[0])
    out.go(wbuf.at[left, first], wbuf.at[left, first], w_sem.at[2], to_right)
    out.go(wbuf.at[left, mine], wbuf.at[left, mine], tw_sem.at[1], twin)
    arrived(wbuf.at[right, mine], w_sem.at[1])
    out.go(wbuf.at[right, second], wbuf.at[right, second], w_sem.at[3], to_left)
    out.go(wbuf.at[right, mine], wbuf.at[right, mine], tw_sem.at[2], twin)

    out.go(wo, wo_out.at[x, orow], o_sem.at[0], to_right)
    out.go(wo, wo_out.at[x, orow], o_sem.at[1], to_left)
    out.go(wo, wo_out.at[x, orow], ot_sem.at[0], twin)
    pltpu.make_async_copy(wo, wo_out.at[x, orow], loc.at[2]).start()

    arrived(wbuf.at[left, theirs], tw_sem.at[1])
    multiply(left, False)
    arrived(wbuf.at[right, theirs], tw_sem.at[2])
    multiply(right, False)
    arrived(wbuf.at[across, first], w_sem.at[2])
    out.go(wbuf.at[across, first], wbuf.at[across, first], tw_sem.at[3], twin)
    arrived(wbuf.at[across, second], w_sem.at[3])
    out.go(wbuf.at[across, second], wbuf.at[across, second], tw_sem.at[4], twin)
    t_first = pl.ds(base_t, half)
    t_second = pl.ds(pl.multiple_of(base_t + half, 16), half)
    arrived(wbuf.at[across, t_first], tw_sem.at[3])
    arrived(wbuf.at[across, t_second], tw_sem.at[4])
    multiply(across, False)

    part[...] = acc[...].astype(part.dtype).reshape(part.shape)
    for peer, device in zip(peers, others):
        out.go(part.at[peer], red.at[y], r_sem.at[y], device)
    red[y] = part[y]
    for peer in peers:
        arrived(red.at[peer], r_sem.at[peer])
    total = red[0].astype(jnp.float32)
    for chip in range(1, ny):
        total = total + red[chip].astype(jnp.float32)

    heads = qcols // 128
    gain = qg[...].astype(jnp.float32)
    for head in range(heads):
        value = norm(total[:, 128 * head : 128 * head + 128], gain)
        for b in range(batch):
            qf[b, 8 * head : 8 * head + 8, :] = value[8 * b : 8 * b + 8]
    qscr[n] = qf[...].astype(qscr.dtype)
    for device in others:
        out.go(qscr.at[n], qscr.at[n], q_sem.at[n], device)
    out.go(qscr.at[n], qscr.at[n], q_sem.at[n], twin)

    keys = norm(total[:, qcols : qcols + kcols], kg[...].astype(jnp.float32))
    values = total[:, qcols + kcols :]
    blank = jnp.zeros((8, 128), jnp.float32)
    for b in range(batch):
        k_out[b] = jnp.concatenate([keys[8 * b : 8 * b + 8], blank], 0).astype(k_out.dtype)
        v_out[b] = jnp.concatenate([values[8 * b : 8 * b + 8], blank], 0).astype(v_out.dtype)

    for peer in peers:
        spot = qscr.at[2 * peer + c]
        arrived(spot, q_sem.at[2 * peer + c])
        out.go(spot, spot, q_sem.at[2 * peer + c], twin)

    arrived(wo_out.at[left, orow], o_sem.at[0])
    out.go(wo_out.at[left, ofirst], wo_out.at[left, ofirst], o_sem.at[2], to_right)
    out.go(wo_out.at[left, orow], wo_out.at[left, orow], ot_sem.at[1], twin)
    arrived(wo_out.at[right, orow], o_sem.at[1])
    out.go(wo_out.at[right, osecond], wo_out.at[right, osecond], o_sem.at[3], to_left)
    out.go(wo_out.at[right, orow], wo_out.at[right, orow], ot_sem.at[2], twin)

    for chip in range(ny):
        spot = qscr.at[2 * chip + 1 - c]
        arrived(spot, q_sem.at[2 * chip + 1 - c])
    q_out[...] = qscr[...]

    arrived(wo_out.at[across, ofirst], o_sem.at[2])
    arrived(wo_out.at[across, osecond], o_sem.at[3])
    out.go(wo_out.at[across, orow], wo_out.at[across, orow], ot_sem.at[3], twin)
    arrived(wo_out.at[x, orow], loc.at[2])
    arrived(wo_out.at[x, orow_t], ot_sem.at[0])
    arrived(wo_out.at[left, orow_t], ot_sem.at[1])
    arrived(wo_out.at[right, orow_t], ot_sem.at[2])
    arrived(wo_out.at[across, orow_t], ot_sem.at[3])
    out.finish()


def project(px, ny, hid, wq, wk, wv, wo, qg, kg, interpret=False):
    nn = 2 * ny
    rows = hid.shape[0]
    batch = rows // 8
    depth = wq.shape[0]
    cols = wq.shape[1] + wk.shape[1] + wv.shape[1]
    heads = wq.shape[1] // 128
    window = 2 * depth + 64
    any_spec = pl.BlockSpec(memory_space=pl.ANY)
    vmem = pl.BlockSpec(memory_space=pltpu.VMEM)
    dma = pltpu.SemaphoreType.DMA
    return pl.pallas_call(
        functools.partial(project_kernel, px, ny, batch),
        out_shape=(
            jax.ShapeDtypeStruct((nn, batch, 8 * heads, 128), jnp.bfloat16),
            jax.ShapeDtypeStruct((batch, 16, 128), jnp.bfloat16),
            jax.ShapeDtypeStruct((batch, 16, 128), jnp.bfloat16),
            jax.ShapeDtypeStruct((px, 2 * depth, wo.shape[1]), jnp.bfloat16),
        ),
        in_specs=[any_spec] * 5 + [vmem] * 2,
        out_specs=(vmem, vmem, vmem, any_spec),
        scratch_shapes=[
            pltpu.VMEM((px, window, cols), jnp.bfloat16),
            pltpu.VMEM((ny, px, rows, window), jnp.bfloat16),
            pltpu.VMEM((ny * rows, cols), jnp.float32),
            pltpu.VMEM((ny, rows, cols), jnp.bfloat16),
            pltpu.VMEM((ny, rows, cols), jnp.bfloat16),
            pltpu.VMEM((batch, 8 * heads, 128), jnp.float32),
            pltpu.VMEM((nn, batch, 8 * heads, 128), jnp.bfloat16),
            dma((80,)),
            dma((3,)),
            dma((4,)),
            dma((5,)),
            dma((ny,)),
            dma((ny,)),
            dma((nn,)),
            dma((4,)),
            dma((4,)),
        ],
        compiler_params=pltpu.CompilerParams(
            collective_id=0, has_side_effects=True, vmem_limit_bytes=48 * 2**20
        ),
        name="project",
    )(hid, wq, wk, wv, wo, qg, kg)


def lanes_of(column, groups):
    shape = (groups * 64, 128)
    row = lax.rem(lax.broadcasted_iota(jnp.int32, shape, 0), 64)
    lane = lax.broadcasted_iota(jnp.int32, shape, 1)
    spread = jnp.where(row == lane, jnp.broadcast_to(column, shape), 0.0)
    return jnp.sum(spread.reshape(groups, 64, 128), axis=1)


def attend_kernel(
    chunk, scale,
    lengths, windows, q_ref, k_ref, v_ref, gk_ref, gv_ref, kn_ref, vn_ref,
    o_ref, l_ref, ow_ref, lw_ref,
):
    b = pl.program_id(0)
    n = lax.axis_index("prefix")
    nn, _, rows, dim = q_ref.shape
    keys_here = k_ref.shape[1]
    rate = scale * LOG2E
    q = q_ref[:, b].reshape(nn * rows, dim)
    valid = lengths[b] - n * keys_here
    top = acc = total = None
    for lo in range(0, keys_here, chunk):
        k = k_ref[0, lo : lo + chunk]
        v = v_ref[0, lo : lo + chunk]
        s = lax.dot_general(q, k, NT, preferred_element_type=jnp.float32)
        at = lo + lax.broadcasted_iota(jnp.int32, (1, chunk), 1)
        s = s + jnp.where(at < valid, 0.0, -1e30)
        here = jnp.max(s, axis=-1, keepdims=True)
        if top is None:
            new = here
        else:
            new = jnp.maximum(top, here)
        w = jnp.exp2((s - new) * rate)
        add = jnp.sum(w, axis=-1, keepdims=True)
        val = jnp.dot(w.astype(jnp.bfloat16), v, preferred_element_type=jnp.float32)
        if top is None:
            total, acc = add, val
        else:
            factor = jnp.exp2((top - new) * rate)
            total, acc = total * factor + add, acc * factor + val
        top = new
    o_ref[:, b] = (acc / total).astype(o_ref.dtype).reshape(nn, rows, dim)
    lse = lanes_of(top * rate + jnp.log2(total), nn)
    for i in range(nn):
        l_ref[i, pl.ds(b, 1), :] = lse[i : i + 1]

    q = q_ref[n, b]
    wide = gk_ref.shape[1]
    s1 = lax.dot_general(q, gk_ref[0], NT, preferred_element_type=jnp.float32)
    s2 = lax.dot_general(q, kn_ref[0], NT, preferred_element_type=jnp.float32)
    row = lax.rem(lax.broadcasted_iota(jnp.int32, (rows, 1), 0), 8)
    sample, step = lax.div(row, 4), lax.rem(row, 4)
    col = lax.broadcasted_iota(jnp.int32, (1, wide), 1)
    whose = (col >= wide // 2).astype(jnp.int32)
    limit = jnp.where(whose == 0, windows[b, 0], windows[b, 1] + wide // 2)
    s1 = jnp.where((whose == sample) & (col < limit), s1, -1e30)
    col = lax.broadcasted_iota(jnp.int32, (1, 16), 1)
    s2 = jnp.where((lax.div(col, 4) == sample) & (lax.rem(col, 4) <= step), s2, -1e30)
    top = jnp.maximum(jnp.max(s1, axis=-1, keepdims=True), jnp.max(s2, axis=-1, keepdims=True))
    w1 = jnp.exp2((s1 - top) * rate)
    w2 = jnp.exp2((s2 - top) * rate)
    total = jnp.sum(w1, axis=-1, keepdims=True) + jnp.sum(w2, axis=-1, keepdims=True)
    acc = jnp.dot(w1.astype(jnp.bfloat16), gv_ref[0], preferred_element_type=jnp.float32)
    acc = acc + jnp.dot(w2.astype(jnp.bfloat16), vn_ref[0], preferred_element_type=jnp.float32)
    ow_ref[b] = acc / total
    lw_ref[pl.ds(b, 1), :] = lanes_of(top * rate + jnp.log2(total), 1)


def attend(lengths, windows, q, keys, values, gen_keys, gen_values, k_new, v_new):
    nn, batch, rows, dim = q.shape
    whole = keys.shape[1]
    wide = gen_keys.shape[1]
    smem = pl.BlockSpec(memory_space=pltpu.SMEM)
    full = lambda shape: pl.BlockSpec(shape, lambda b: (0,) * len(shape))
    each = lambda shape: pl.BlockSpec(shape, lambda b: (b, 0, 0))
    return pl.pallas_call(
        functools.partial(attend_kernel, min(1024, whole), 1.0 / math.sqrt(dim)),
        grid=(batch,),
        out_shape=(
            jax.ShapeDtypeStruct((nn, batch, rows, dim), jnp.bfloat16),
            jax.ShapeDtypeStruct((nn, 8, 128), jnp.float32),
            jax.ShapeDtypeStruct((batch, rows, dim), jnp.float32),
            jax.ShapeDtypeStruct((8, 128), jnp.float32),
        ),
        in_specs=[
            smem,
            smem,
            full((nn, batch, rows, dim)),
            each((1, whole, dim)),
            each((1, whole, dim)),
            each((1, wide, dim)),
            each((1, wide, dim)),
            each((1, 16, dim)),
            each((1, 16, dim)),
        ],
        out_specs=(
            full((nn, batch, rows, dim)),
            full((nn, 8, 128)),
            full((batch, rows, dim)),
            full((8, 128)),
        ),
        compiler_params=pltpu.CompilerParams(vmem_limit_bytes=48 * 2**20),
        name="attend",
    )(lengths, windows, q, keys, values, gen_keys, gen_values, k_new, v_new)


def finish_kernel(
    px, ny, nz, batch,
    o_in, l_in, ow, lw, wo_in,
    out_ref,
    o_rcv, l_rcv, wbuf, attf, att, msg, rcv,
    send, loc, o_sem, l_sem, a_sem, m_sem,
):
    nn = 2 * ny
    x = lax.axis_index("prompt")
    n = lax.axis_index("prefix")
    z = lax.axis_index("sample")
    y, c = lax.div(n, 2), lax.rem(n, 2)
    per = px * nn // nz
    heads = att.shape[2] // 128

    def home(block, chip):
        return lax.div(block * nn + 2 * chip, per)

    first_chip = lax.div(lax.rem(per * z, nn), 2)

    barrier = pltpu.get_barrier_semaphore()
    prefix_peers = [lax.rem(n + i, nn) for i in range(1, nn)]
    for peer in prefix_peers:
        pl.semaphore_signal(barrier, inc=1, device_id={"prefix": peer}, device_id_type=MESH)
    for k in range(2):
        for zz in range(nz):
            chip = first_chip + k

            @pl.when(jnp.logical_or(chip != y, zz != z))
            def _():
                pl.semaphore_signal(
                    barrier,
                    inc=1,
                    device_id={"prefix": 2 * chip + c, "sample": zz},
                    device_id_type=MESH,
                )

    pltpu.make_async_copy(wo_in, wbuf, loc.at[0]).start()
    pltpu.make_async_copy(o_in.at[n], o_rcv.at[n], loc.at[1]).start()
    pltpu.make_async_copy(l_in.at[n], l_rcv.at[n], loc.at[2]).start()
    mine = jnp.int32(0)
    for block in range(px):
        mine = mine + (home(block, y) == z).astype(jnp.int32)
    pl.semaphore_wait(barrier, nn - 1 + px * ny - mine)

    out = Sends(send)
    for peer in prefix_peers:
        device = {"prefix": peer}
        out.go(l_in.at[peer], l_rcv.at[n], l_sem.at[n], device)
        out.go(o_in.at[peer], o_rcv.at[n], o_sem.at[n], device)
    arrived(o_rcv.at[n], loc.at[1])
    arrived(l_rcv.at[n], loc.at[2])
    for peer in prefix_peers:
        arrived(l_rcv.at[peer], l_sem.at[peer])
        arrived(o_rcv.at[peer], o_sem.at[peer])

    own = lw[...]
    top = own
    for i in range(nn):
        top = jnp.maximum(top, l_rcv[i])
    parts = [jnp.exp2(l_rcv[i] - top) for i in range(nn)] + [jnp.exp2(own - top)]
    inverse = 1.0 / sum(parts[1:], parts[0])
    parts = [part * inverse for part in parts]
    row = lax.broadcasted_iota(jnp.int32, (64, 128), 0)
    lane = lax.broadcasted_iota(jnp.int32, (64, 128), 1)
    pick = row == lane
    for b in range(batch):
        total = None
        for i in range(nn + 1):
            weight = jnp.broadcast_to(parts[i][b : b + 1], (64, 128))
            weight = jnp.sum(jnp.where(pick, weight, 0.0), axis=-1, keepdims=True)
            value = ow[b] if i == nn else o_rcv[i, b].astype(jnp.float32)
            total = weight * value if total is None else total + weight * value
        for head in range(heads):
            attf[8 * b : 8 * b + 8, 128 * head : 128 * head + 128] = total[
                8 * head : 8 * head + 8
            ]
    att[y] = attf[...].astype(att.dtype)
    peers = [lax.rem(y + i, ny) for i in range(1, ny)]
    for peer in peers:
        out.go(att.at[y], att.at[y], a_sem.at[y], {"prefix": 2 * peer + c})
    arrived(wbuf, loc.at[0])
    for peer in peers:
        arrived(att.at[peer], a_sem.at[peer])

    odd = lax.rem(y, 2)
    rows = att.shape[1]
    lhs = att[...].reshape(ny * rows, att.shape[2])
    lane = lax.broadcasted_iota(jnp.int32, (16, 128), 1)
    for block in range(px):
        main = wbuf[block, pl.ds(pl.multiple_of(64 * odd, 64), 256), :]
        rest = wbuf[block, pl.ds(pl.multiple_of(256 * (1 - odd), 64), 64), :]
        rest = jnp.concatenate([rest, rest], 0)
        main = lax.dot_general(lhs, main, NT, preferred_element_type=jnp.float32)
        rest = lax.dot_general(lhs, rest, NT, preferred_element_type=jnp.float32)
        for chip in range(ny):
            r = rows * chip
            msg[block, chip, 0:32, :] = main[r : r + 32, 0:128].astype(msg.dtype)
            msg[block, chip, 32:64, :] = main[r : r + 32, 128:256].astype(msg.dtype)
            low, high = rest[r : r + 16], rest[r + 16 : r + 32]
            msg[block, chip, 64:80, :] = jnp.where(lane < 64, low, high).astype(msg.dtype)
        target = home(block, y)
        for i in range(ny):
            chip = lax.rem(y + i, ny)
            copy = pltpu.make_async_remote_copy(
                src_ref=msg.at[block, chip],
                dst_ref=rcv.at[odd, z],
                send_sem=send.at[60 + block * ny + i],
                recv_sem=m_sem.at[odd, z],
                device_id={"prefix": 2 * chip + c, "sample": target},
                device_id_type=MESH,
            )
            if i > 0:
                copy.start()
            else:

                @pl.when(target != z)
                def _():
                    copy.start()

                @pl.when(target == z)
                def _():
                    rcv[odd, z] = msg[block, chip]

    for k in range(2):
        chip = first_chip + k
        for i in range(nz):
            zz = lax.rem(z + i, nz)
            if i > 0:
                arrived(rcv.at[k, zz], m_sem.at[k, zz])
            else:

                @pl.when(chip != y)
                def _():
                    arrived(rcv.at[k, zz], m_sem.at[k, zz])

    sums = []
    for k in range(2):
        total = rcv[k, 0].astype(jnp.float32)
        for zz in range(1, nz):
            total = total + rcv[k, zz].astype(jnp.float32)
        sums.append(total)
    a, d = sums
    out_ref[:, 0:128] = a[0:32].astype(out_ref.dtype)
    out_ref[:, 128:256] = a[32:64].astype(out_ref.dtype)
    a, e = a[64:80], d[64:80]
    low = jnp.where(lane < 64, a, pltpu.roll(e, 64, 1))
    high = jnp.where(lane < 64, pltpu.roll(a, 64, 1), e)
    out_ref[0:16, 256:384] = low.astype(out_ref.dtype)
    out_ref[16:32, 256:384] = high.astype(out_ref.dtype)
    out_ref[:, 384:512] = d[0:32].astype(out_ref.dtype)
    out_ref[:, 512:640] = d[32:64].astype(out_ref.dtype)

    out.finish()
    for block in range(px):
        target = home(block, y)
        for i in range(ny):
            chip = lax.rem(y + i, ny)
            copy = pltpu.make_async_remote_copy(
                src_ref=msg.at[block, chip],
                dst_ref=rcv.at[odd, z],
                send_sem=send.at[60 + block * ny + i],
                recv_sem=m_sem.at[odd, z],
                device_id={"prefix": 2 * chip + c, "sample": target},
                device_id_type=MESH,
            )
            if i > 0:
                copy.wait_send()
            else:

                @pl.when(target != z)
                def _():
                    copy.wait_send()


def finish(px, ny, nz, o, lse, o_win, lse_win, wo):
    nn, batch, rows, dim = o.shape
    tokens = 8 * batch
    width = wo.shape[2]
    any_spec = pl.BlockSpec(memory_space=pl.ANY)
    vmem = pl.BlockSpec(memory_space=pltpu.VMEM)
    dma = pltpu.SemaphoreType.DMA
    return pl.pallas_call(
        functools.partial(finish_kernel, px, ny, nz, batch),
        out_shape=jax.ShapeDtypeStruct((tokens, 640), jnp.bfloat16),
        in_specs=[any_spec, any_spec, vmem, vmem, any_spec],
        out_specs=vmem,
        scratch_shapes=[
            pltpu.VMEM(o.shape, jnp.bfloat16),
            pltpu.VMEM(lse.shape, jnp.float32),
            pltpu.VMEM(wo.shape, jnp.bfloat16),
            pltpu.VMEM((tokens, width), jnp.float32),
            pltpu.VMEM((ny, tokens, width), jnp.bfloat16),
            pltpu.VMEM((px, ny, 80, 128), jnp.bfloat16),
            pltpu.VMEM((2, nz, 80, 128), jnp.bfloat16),
            dma((60 + px * ny,)),
            dma((3,)),
            dma((nn,)),
            dma((nn,)),
            dma((ny,)),
            dma((2, nz)),
        ],
        compiler_params=pltpu.CompilerParams(
            collective_id=1, has_side_effects=True, vmem_limit_bytes=48 * 2**20
        ),
        name="finish",
    )(o, lse, o_win, lse_win, wo)


def on_device(
    px, ny, nz,
    new_hidden, query_projection_weight, key_projection_weight, value_projection_weight, w_out,
    query_norm_gain, key_norm_gain, prefix_keys, prompt_cache_values,
    generated_keys, generated_values, prompt_lengths, window_lengths,
):
    batch, samples, steps, width = new_hidden.shape
    dim = query_norm_gain.shape[0]
    q, k_new, v_new, wo = project(
        px,
        ny,
        new_hidden.reshape(batch * samples * steps, width),
        query_projection_weight,
        key_projection_weight,
        value_projection_weight,
        w_out.T,
        query_norm_gain.reshape(1, dim),
        key_norm_gain.reshape(1, dim),
    )
    o, lse, o_win, lse_win = attend(
        prompt_lengths,
        window_lengths,
        q,
        prefix_keys.reshape(batch, -1, dim),
        prompt_cache_values.reshape(batch, -1, dim),
        generated_keys.reshape(batch, -1, dim),
        generated_values.reshape(batch, -1, dim),
        k_new,
        v_new,
    )
    block = finish(px, ny, nz, o, lse, o_win, lse_win, wo)
    return block.reshape(batch, samples, steps, -1)


def solution(mesh):
    sizes = mesh.shape
    body = functools.partial(
        on_device, sizes["prompt"], sizes["prefix"] // 2, sizes["sample"]
    )
    return jax.shard_map(
        body,
        mesh=mesh,
        in_specs=(
            P("prompt", "prefix", None, None),
            P(("prompt", "prefix"), "sample"),
            P(("prompt", "prefix"), "sample"),
            P(("prompt", "prefix"), "sample"),
            P("sample", ("prompt", "prefix")),
            P(),
            P(),
            P("prompt", "prefix", "sample", None),
            P("prompt", "prefix", "sample", None),
            P("prompt", "prefix", None, "sample", None),
            P("prompt", "prefix", None, "sample", None),
            P("prompt"),
            P("prompt", "prefix"),
        ),
        out_specs=P("prompt", "prefix", None, "sample"),
        check_vma=False,
    )
```

time: 400 us -> 105 us (0.26)
  waiting for transfers between devices: 209 us -> 0 us
  blocking collectives: 98.4 us -> 0 us
  Pallas kernels: 0 us -> 94 us
  matrix products: 40.8 us -> 0 us
  other arithmetic: 19.3 us -> 0 us
  between operations: 14 us -> 0.06 us
  local copies, waits for them, and re-layouts: 15.6 us -> 10.4 us
    pallas_call x0 -> x3, Pallas kernels: none -> 94 us  [the longest x1 43.6 us: project(): pl.pallas_call(functools.partial(project_kernel, px, ny, batch), out_shap...]
    reduce_scatter x1 -> x0, waiting for transfers between devices: 86.8 us -> none  [on_device(): lax.psum_scatter(jnp.dot(spread, weights, preferred_element_type=jnp.floa...]
    unnamed x6 -> x0, waiting for transfers between devices: 73.8 us -> none
    all_gather x1 -> x0, waiting for transfers between devices: 48.8 us -> none  [on_device(): lax.all_gather(attended, ('prompt', 'prefix'), axis=0, tiled=True)]
    dot_general x8 -> x0, matrix products: 40.8 us -> none  [the longest x1 15.9 us: on_device(): jnp.einsum('psrhgn,pnhd->psrhgd', weight.astype(jnp.bfloat16), prompt_cac...]
    all_to_all x2 -> x0, blocking collectives: 34.4 us -> none  [the longest x1 18.3 us: on_device(): lax.all_to_all(token_matrix, ('prompt', 'prefix'), split_axis=1, concat_a...]
    pmax x1 -> x0, blocking collectives: 27 us -> none  [on_device(): global_top = lax.pmax(local_top, 'prefix')]
    unnamed x1 -> x0, blocking collectives: 23.9 us -> none
  transfers between devices with their start and end apart: 4 -> 0, of which waited for: 4 -> 0; matrix products, arithmetic and copies ran while one was open for 2% -> 0% of each run, Pallas kernels for 0% -> 0%
where the time goes in v1:
time: 105 us; the launch traced here: 104 us
  Pallas kernels  94 us (90%)
  local copies, waits for them, and re-layouts  10.4 us (10%)
    pallas_call x1, Pallas kernels, project(): pl.pallas_call(functools.partial(project_kernel, px, ny, batch), out_shap...  43.6 us
    pallas_call x1, Pallas kernels, finish(): pl.pallas_call(functools.partial(finish_kernel, px, ny, nz, batch), out_s...  34.9 us
    pallas_call x1, Pallas kernels, attend(): pl.pallas_call(functools.partial(attend_kernel, min(1024, whole), 1.0 / m...  15.5 us
    unnamed x19, local copies, waits for them, and re-layouts  8.67 us

profile of v1, /device:TPU:32, one launch (start us, length us, event | category | flops | bytes accessed | tf_op | source)
XLA Modules:
  0.0 104.4 jit_solution(2954420288599201542)
XLA Ops:
  0.0 0.8 copy.14.windows
  0.8 1.0 %reshape.24.hid = bf16[32,5120]{1,0:T(8,128)(2,1)S(1)} reshape(bf16[4,2,4,5120]{3,2,1,0:T(4,128)(2,1)} %param.13) | data formatting | bytes 655360 | tf_op jit(solution)/shard_map/reshape | solution.py:594
  1.8 0.0 copy-start.2
  1.8 1.0 copy-done.2
  2.8 0.0 copy-start.3
  2.8 1.0 copy-done.3
  3.8 0.0 copy-start.4
  3.8 0.8 copy-done.4
  4.5 0.0 copy-start.5
  4.5 0.8 copy-done.5
  5.3 0.0 copy-start.6
  5.3 0.7 copy-done.6
  6.0 0.0 copy-start.7
  6.0 0.7 copy-done.7
  6.6 43.6 %project.1 = (bf16[8,4,64,128]{3,2,1,0:T(8,128)(2,1)S(1)}, bf16[4,16,128]{2,1,0:T(8,128)(2,1)S(1)}, bf16[4,16,128]{2,1,0:T(8,128)(2,1)S(1)}, bf16[4,320,1024]{2,1,0:T(8,128)(2,1)S(1)}) custom-call(bf16[32,5120]{1,0:T(8,128)(2,1)S(1)} %reshape.24.hid, bf16[160,1024]{1,0:T(8,128)(2,1)S(1)} %copy-done.2, bf16[160,128]{1,0:T(8,128)(2,1)S(1)} %copy-done.4, ...), custom_call_target="tpu_custom_call" | custom-call | tf_op jit(solution)/shard_map/project/pallas_call | solution.py:233
  50.3 0.0 copy-start
  50.3 1.2 %copy-done = bf16[4,2,512,1,128]{4,2,3,1,0:T(8,128)(2,1)S(1)} copy-done((bf16[4,2,512,1,128]{4,2,3,1,0:T(8,128)(2,1)S(1)}, bf16[4,2,512,1,128]{4,2,3,1,0:T(8,128)(2,1)}, u32[]{:S(2)}) %copy-start) | copy-done | bytes 1048600
  51.5 0.0 copy-start.1
  51.5 1.2 %copy-done.1 = bf16[4,2,512,1,128]{4,2,3,1,0:T(8,128)(2,1)S(1)} copy-done((bf16[4,2,512,1,128]{4,2,3,1,0:T(8,128)(2,1)S(1)}, bf16[4,2,512,1,128]{4,2,3,1,0:T(8,128)(2,1)}, u32[]{:S(2)}) %copy-start.1) | copy-done | bytes 1048600
  52.7 0.0 copy-start.8
  52.7 0.7 copy-done.8
  53.4 15.5 %attend.1 = (bf16[8,4,64,128]{3,2,1,0:T(8,128)(2,1)S(1)}, f32[8,8,128]{2,1,0:T(8,128)S(1)}, f32[4,64,128]{2,1,0:T(8,128)S(1)}, f32[8,128]{1,0:T(8,128)S(1)}) custom-call(s32[4]{0:T(128)S(1)} %copy-done.8, s32[4,2]{1,0:T(4,128)S(1)} %copy.14.windows, bf16[8,4,64,128]{3,2,1,0:T(8,128)(2,1)S(1)} %get-tuple-element.13.q_ref, bf16[4,4096,128]{2,1,0:T(8,128)(2,1)} %bitcast.12, ...), custom_call_target="tpu_custom_call" | custom-call | tf_op jit(solution)/shard_map/attend/pallas_call | solution.py:343
  68.9 34.9 %finish.1 = bf16[32,640]{1,0:T(8,128)(2,1)S(1)} custom-call(bf16[8,4,64,128]{3,2,1,0:T(8,128)(2,1)S(1)} %get-tuple-element.16.o_in, f32[8,8,128]{2,1,0:T(8,128)S(1)} %get-tuple-element.17.l_in, f32[4,64,128]{2,1,0:T(8,128)S(1)} %get-tuple-element.18.ow, f32[8,128]{1,0:T(8,128)S(1)} %get-tuple-element.19.lw, bf16[4,320,1024]{2,1,0:T(8,128)(2,1)S(1)} %get-tuple-element.20.wo_in), custom_call_target="tpu_custom_call" | custom-call | tf_op jit(solution)/shard_map/finish/pallas_call | solution.py:556
  103.8 0.6 reshape.31
Async XLA Ops:
  1.8 1.0 copy-start.2
  2.8 1.0 copy-start.3
  3.8 0.8 copy-start.4
  4.5 0.8 copy-start.5
  5.3 0.7 copy-start.6
  6.0 0.7 copy-start.7
  50.3 1.2 %copy-start = (bf16[4,2,512,1,128]{4,2,3,1,0:T(8,128)(2,1)S(1)}, bf16[4,2,512,1,128]{4,2,3,1,0:T(8,128)(2,1)}, u32[]{:S(2)}) copy-start(bf16[4,2,512,1,128]{4,2,3,1,0:T(8,128)(2,1)} %param.22) | copy-start | bytes 3145732
  51.5 1.2 %copy-start.1 = (bf16[4,2,512,1,128]{4,2,3,1,0:T(8,128)(2,1)S(1)}, bf16[4,2,512,1,128]{4,2,3,1,0:T(8,128)(2,1)}, u32[]{:S(2)}) copy-start(bf16[4,2,512,1,128]{4,2,3,1,0:T(8,128)(2,1)} %param.23) | copy-start | bytes 3145732
  52.7 0.7 copy-start.8

commit v2 on v0

v2 whole, which is shorter than its diff:
```python
import functools
import math

import jax
import jax.numpy as jnp
from jax import lax
from jax.experimental import pallas as pl
from jax.experimental.pallas import tpu as pltpu
from jax.sharding import PartitionSpec as P

MESH = pl.DeviceIdType.MESH
LOG2E = 1.4426950408889634
NT = (((1,), (1,)), ((), ()))
TN = (((0,), (0,)), ((), ()))
CHUNK = 1024


class Sends:
    def __init__(self, sems):
        self.sems = sems
        self.started = []

    def go(self, src, dst, recv, device, when=None):
        copy = pltpu.make_async_remote_copy(
            src_ref=src,
            dst_ref=dst,
            send_sem=self.sems.at[len(self.started)],
            recv_sem=recv,
            device_id=device,
            device_id_type=MESH,
        )
        if when is None:
            copy.start()
        else:
            pl.when(when)(copy.start)
        self.started.append((copy, when))

    def finish(self):
        for copy, when in self.started:
            if when is None:
                copy.wait_send()
            else:
                pl.when(when)(copy.wait_send)


def arrived(ref, sem):
    pltpu.make_async_copy(ref, ref, sem).wait()


def norm(raw, gain):
    scale = lax.rsqrt(jnp.mean(raw * raw, axis=-1, keepdims=True) + 1e-06)
    return raw * scale * gain


def lanes_of(column, count):
    shape = (count, 128)
    row = lax.broadcasted_iota(jnp.int32, shape, 0)
    lane = lax.broadcasted_iota(jnp.int32, shape, 1)
    spread = jnp.where(row == lane, jnp.broadcast_to(column, shape), 0.0)
    return jnp.sum(spread, axis=0, keepdims=True)


def kernel(
    px, ny, nz,
    lengths, windows, hid, wq, wk, wv, wo, qg, kg, keys, values, gkeys, gvalues,
    out_ref,
    kbuf, vbuf, gkb, gvb, wbuf, obuf, tok, acc, part_a, part_b, red_a, red_b,
    qf, qa, qb, kn, vn, pa, pb, la, lb, ra, rb, sa, sb, ow, lw, attf, att, msg, rcv,
    send, loc, w_sem, tw_sem, t_sem, r_sem, q_sem, o_sem, ot_sem, p_sem, s_sem, a_sem, m_sem,
):
    nn = 2 * ny
    x = lax.axis_index("prompt")
    n = lax.axis_index("prefix")
    z = lax.axis_index("sample")
    y, c = lax.div(n, 2), lax.rem(n, 2)
    odd = lax.rem(y, 2)
    right, left = lax.rem(x + 1, px), lax.rem(x + px - 1, px)
    across = lax.rem(x + 2, px)
    rows, width = hid.shape
    batch = keys.shape[0]
    keys_here = keys.shape[1]
    depth = wq.shape[0]
    qcols, kcols = wq.shape[1], wk.shape[1]
    cols = qcols + 2 * kcols
    cut = qcols // 2
    pair = 2 * depth
    window = wbuf.shape[1]
    pad = window - pair
    heads = qcols // 128
    hh = heads // 2
    gr = 8 * hh
    rate = LOG2E / math.sqrt(128)
    twin = {"prefix": 2 * y + 1 - c}
    peers = [lax.rem(y + i, ny) for i in range(1, ny)]
    others = [{"prefix": 2 * peer + c} for peer in peers]
    prefix_peers = [lax.rem(n + i, nn) for i in range(1, nn)]
    x_targets = [{"prompt": right}, {"prompt": left}, {"prompt": across}]
    x_sources = [left, right, across]
    per = px * nn // nz

    def home(block, chip):
        return lax.div(block * nn + 2 * chip, per)

    first_chip = lax.div(lax.rem(per * z, nn), 2)

    for i, (src, dst) in enumerate(
        ((keys, kbuf), (values, vbuf), (gkeys, gkb), (gvalues, gvb))
    ):
        pltpu.make_async_copy(src, dst, loc.at[3 + i]).start()
    zero = jnp.zeros((px, pad, cols), wbuf.dtype)
    wbuf[:, 0:pad, :] = zero
    wbuf[:, pair : pair + pad, :] = zero

    barrier = pltpu.get_barrier_semaphore()
    greeted = x_targets + [{"prefix": peer} for peer in prefix_peers]
    for device in greeted:
        pl.semaphore_signal(barrier, inc=1, device_id=device, device_id_type=MESH)
    for k in range(2):
        chip = first_chip + k
        for zz in range(nz):

            @pl.when(jnp.logical_or(chip != y, zz != z))
            def _():
                pl.semaphore_signal(
                    barrier,
                    inc=1,
                    device_id={"prefix": 2 * chip + c, "sample": zz},
                    device_id_type=MESH,
                )

    mine_too = jnp.int32(0)
    for block in range(px):
        mine_too = mine_too + (home(block, y) == z).astype(jnp.int32)
    pl.semaphore_wait(barrier, len(greeted) + px * ny - mine_too)

    out = Sends(send)
    base = pl.multiple_of(pad * odd + depth * c, 16)
    mine = pl.ds(base, depth)
    theirs = pl.ds(pl.multiple_of(pad * odd + depth * (1 - c), 16), depth)
    group_a = ((wq.at[:, 0:cut], 0, cut),)
    group_b = (
        (wq.at[:, cut:qcols], cut, qcols - cut),
        (wk, qcols, kcols),
        (wv, qcols + kcols, kcols),
    )
    spans = (slice(0, cut), slice(cut, cols))

    def send_weights(group, which):
        for piece, lo, size in (group_a, group_b)[group]:
            spot = wbuf.at[x, mine, lo : lo + size]
            if which == 3:
                out.go(piece, spot, tw_sem.at[group, 3], twin)
            elif which == 4:
                pltpu.make_async_copy(piece, spot, loc.at[group]).start()
            else:
                out.go(piece, spot, w_sem.at[group, which], x_targets[which])

    def start_of(block, chip):
        return pl.multiple_of(128 * lax.div(pair * ny * block + pair * chip, 128), 128)

    for which in range(3):
        send_weights(0, which)
    for peer, device in zip(peers, others):
        for block in range(px):
            out.go(
                hid.at[:, pl.ds(start_of(block, peer), window)],
                tok.at[y, block],
                t_sem.at[y],
                device,
            )
    send_weights(0, 3)
    send_weights(0, 4)
    for block in range(px):
        pltpu.make_async_copy(
            hid.at[:, pl.ds(start_of(block, y), window)], tok.at[y, block], loc.at[2]
        ).start()
    send_weights(1, 3)
    send_weights(1, 4)

    def multiply(block, group, start):
        span = spans[group]
        lhs = tok[:, block].reshape(ny * rows, window)
        value = jnp.dot(lhs, wbuf[block, :, span], preferred_element_type=jnp.float32)
        if start:
            acc[:, span] = value
        else:
            acc[:, span] += value

    orow = pl.ds(pl.multiple_of(depth * c, 16), depth)
    orow_t = pl.ds(pl.multiple_of(depth * (1 - c), 16), depth)

    def project(group, after):
        span = spans[group]
        arrived(wbuf.at[x, mine, span], loc.at[group])
        if group == 0:
            arrived(tok.at[y], loc.at[2])
            for peer in peers:
                arrived(tok.at[peer], t_sem.at[peer])
        arrived(wbuf.at[x, theirs, span], tw_sem.at[group, 3])
        multiply(x, group, True)
        for which, source in enumerate(x_sources):
            spot = wbuf.at[source, mine, span]
            arrived(spot, w_sem.at[group, which])
            out.go(spot, spot, tw_sem.at[group, which], twin)
            after(which)
        for which, source in enumerate(x_sources):
            arrived(wbuf.at[source, theirs, span], tw_sem.at[group, which])
            multiply(source, group, False)
        part, red = ((part_a, red_a), (part_b, red_b))[group]
        part[...] = acc[:, span].astype(part.dtype).reshape(part.shape)
        for peer, device in zip(peers, others):
            out.go(part.at[peer], red.at[y], r_sem.at[group, y], device)
        red[y] = part[y]

    gain = qg[...].astype(jnp.float32)

    def own(group):
        red = (red_a, red_b)[group]
        for peer in peers:
            arrived(red.at[peer], r_sem.at[group, peer])
        total = red[0].astype(jnp.float32)
        for chip in range(1, ny):
            total = total + red[chip].astype(jnp.float32)
        for head in range(hh):
            value = norm(total[:, 128 * head : 128 * head + 128], gain)
            for b in range(batch):
                qf[b, 8 * head : 8 * head + 8, :] = value[8 * b : 8 * b + 8]
        q = (qa, qb)[group]
        q[n] = qf[...].astype(q.dtype)
        for peer in prefix_peers:
            out.go(q.at[n], q.at[n], q_sem.at[group, n], {"prefix": peer})
        return total

    def queries(group):
        q = (qa, qb)[group]
        for peer in prefix_peers:
            arrived(q.at[peer], q_sem.at[group, peer])

    def attend(b, group, store_lse):
        q = (qa, qb)[group][:, b].reshape(nn * gr, 128)
        valid = lengths[b] - n * keys_here
        top = total = value = None
        for lo in range(0, keys_here, CHUNK):
            size = min(CHUNK, keys_here - lo)
            k = kbuf[b, lo : lo + size]
            v = vbuf[b, lo : lo + size]
            s = lax.dot_general(k, q, NT, preferred_element_type=jnp.float32)
            at = lo + lax.broadcasted_iota(jnp.int32, (size, 1), 0)
            s = s + jnp.where(at < valid, 0.0, -1e30)
            here = jnp.max(s, axis=0, keepdims=True)
            new = here if top is None else jnp.maximum(top, here)
            w = jnp.exp2((s - new) * rate)
            add = jnp.sum(w, axis=0, keepdims=True)
            val = lax.dot_general(
                v, w.astype(jnp.bfloat16), TN, preferred_element_type=jnp.float32
            )
            if top is None:
                total, value = add, val
            else:
                factor = jnp.exp2((top - new) * rate)
                total, value = total * factor + add, value * factor + val
            top = new
        p = (pa, pb)[group]
        p[:, b] = (value / total).T.astype(p.dtype).reshape(nn, gr, 128)
        store_lse(top * rate + jnp.log2(total))

    def attend_own(b):
        q = jnp.concatenate([qa[n, b], qb[n, b]], 0)
        wide = gkb.shape[1]
        s1 = lax.dot_general(q, gkb[b], NT, preferred_element_type=jnp.float32)
        s2 = lax.dot_general(q, kn[b], NT, preferred_element_type=jnp.float32)
        row = lax.rem(lax.broadcasted_iota(jnp.int32, (2 * gr, 1), 0), 8)
        sample, step = lax.div(row, 4), lax.rem(row, 4)
        col = lax.broadcasted_iota(jnp.int32, (1, wide), 1)
        whose = (col >= wide // 2).astype(jnp.int32)
        limit = jnp.where(whose == 0, windows[0, b], windows[1, b] + wide // 2)
        s1 = jnp.where((whose == sample) & (col < limit), s1, -1e30)
        col = lax.broadcasted_iota(jnp.int32, (1, 16), 1)
        s2 = jnp.where((lax.div(col, 4) == sample) & (lax.rem(col, 4) <= step), s2, -1e30)
        top = jnp.maximum(
            jnp.max(s1, axis=-1, keepdims=True), jnp.max(s2, axis=-1, keepdims=True)
        )
        w1 = jnp.exp2((s1 - top) * rate)
        w2 = jnp.exp2((s2 - top) * rate)
        total = jnp.sum(w1, axis=-1, keepdims=True) + jnp.sum(w2, axis=-1, keepdims=True)
        value = jnp.dot(w1.astype(jnp.bfloat16), gvb[b], preferred_element_type=jnp.float32)
        value = value + jnp.dot(
            w2.astype(jnp.bfloat16), vn[b], preferred_element_type=jnp.float32
        )
        ow[b] = value / total
        lse = top * rate + jnp.log2(total)
        lw[0, pl.ds(b, 1), :] = lanes_of(lse[0:gr], gr)
        lw[1, pl.ds(b, 1), :] = lanes_of(lse[gr:], gr)

    project(0, lambda which: send_weights(1, which))
    own(0)

    def send_wo(which):
        out.go(wo, obuf.at[x, orow], o_sem.at[which], x_targets[which])

    project(1, send_wo)
    out.go(wo, obuf.at[x, orow], ot_sem.at[3], twin)
    pltpu.make_async_copy(wo, obuf.at[x, orow], loc.at[7]).start()

    arrived(kbuf, loc.at[3])
    arrived(vbuf, loc.at[4])
    queries(0)

    def attend_a(b, _):
        def store(lse):
            la[pl.ds(b, 1), :] = lse

        attend(b, 0, store)
        return 0

    lax.fori_loop(0, batch // 2, attend_a, 0)

    total = own(1)
    q_there = qcols - cut
    k_new = norm(total[:, q_there : q_there + kcols], kg[...].astype(jnp.float32))
    v_new = total[:, q_there + kcols :]
    blank = jnp.zeros((8, 128), jnp.float32)
    for b in range(batch):
        kn[b] = jnp.concatenate([k_new[8 * b : 8 * b + 8], blank], 0).astype(kn.dtype)
        vn[b] = jnp.concatenate([v_new[8 * b : 8 * b + 8], blank], 0).astype(vn.dtype)

    lax.fori_loop(batch // 2, batch, attend_a, 0)
    for peer in prefix_peers:
        out.go(la, sa.at[n], s_sem.at[0, n], {"prefix": peer})
        out.go(pa.at[peer], ra.at[n], p_sem.at[0, n], {"prefix": peer})
    ra[n] = pa[n]
    sa[n] = la[...]

    arrived(gkb, loc.at[5])
    arrived(gvb, loc.at[6])

    def own_body(b, _):
        attend_own(b)
        return 0

    lax.fori_loop(0, batch, own_body, 0)

    for which, source in enumerate(x_sources):
        spot = obuf.at[source, orow]
        arrived(spot, o_sem.at[which])
        out.go(spot, spot, ot_sem.at[which], twin)

    queries(1)
    half = batch // 2

    def attend_b(h):
        def body(i, _):
            def store(lse):
                lb[h, pl.ds(i, 1), :] = lse

            attend(h * half + i, 1, store)
            return 0

        lax.fori_loop(0, half, body, 0)
        span = slice(h * half, h * half + half)
        for peer in prefix_peers:
            device = {"prefix": peer}
            out.go(lb.at[h], sb.at[n, h], s_sem.at[1 + h, n], device)
            out.go(pb.at[peer, span], rb.at[n, h], p_sem.at[1 + h, n], device)
        rb[n, h] = pb[n, span]
        sb[n, h] = lb[h]

    row = lax.broadcasted_iota(jnp.int32, (gr, 128), 0)
    lane = lax.broadcasted_iota(jnp.int32, (gr, 128), 1)
    pick = row == lane
    many = nn * gr

    def merge(h):
        if h == 0:
            for peer in prefix_peers:
                arrived(sa.at[peer], s_sem.at[0, peer])
                arrived(ra.at[peer], p_sem.at[0, peer])
        for peer in prefix_peers:
            arrived(sb.at[peer, h], s_sem.at[1 + h, peer])
            arrived(rb.at[peer, h], p_sem.at[1 + h, peer])
        shift = lax.rem(many - gr * n, many)
        for group in range(2):
            stats = []
            for i in range(nn):
                s = sa[i] if group == 0 else sb[i, h]
                stats.append(pltpu.roll(s, shift, 1)[:, 0:128])
            lo = half * h if group == 0 else 0
            mine_stats = lw[group, half * h : half * h + half, :]
            stats = [s[lo : lo + half] for s in stats] + [mine_stats]
            top = functools.reduce(jnp.maximum, stats)
            parts = [jnp.exp2(s - top) for s in stats]
            inverse = 1.0 / functools.reduce(lambda u, w: u + w, parts)
            parts = [part * inverse for part in parts]
            for i in range(half):
                b = half * h + i
                total = None
                for source in range(nn + 1):
                    weight = jnp.broadcast_to(parts[source][i : i + 1], (gr, 128))
                    weight = jnp.sum(jnp.where(pick, weight, 0.0), axis=-1, keepdims=True)
                    if source == nn:
                        value = ow[b, gr * group : gr * group + gr]
                    elif group == 0:
                        value = ra[source, b].astype(jnp.float32)
                    else:
                        value = rb[source, h, i].astype(jnp.float32)
                    total = weight * value if total is None else total + weight * value
                for head in range(hh):
                    at = 128 * (hh * group + head)
                    attf[8 * i : 8 * i + 8, at : at + 128] = total[8 * head : 8 * head + 8]
        att[h, y] = attf[...].astype(att.dtype)
        for device in others:
            out.go(att.at[h, y], att.at[h, y], a_sem.at[h, y], device)

    lane8 = lax.broadcasted_iota(jnp.int32, (8, 128), 1)

    def output(h):
        for peer in peers:
            arrived(att.at[h, peer], a_sem.at[h, peer])
        lhs = att[h].reshape(ny * 16, att.shape[3])
        blank = jnp.zeros((8, 128), jnp.float32)
        for block in range(px):
            main = obuf[block, pl.ds(pl.multiple_of(64 * odd, 64), 256), :]
            rest = obuf[block, pl.ds(pl.multiple_of(256 * (1 - odd), 64), 64), :]
            rest = jnp.concatenate([rest, rest], 0)
            main = lax.dot_general(lhs, main, NT, preferred_element_type=jnp.float32)
            rest = lax.dot_general(lhs, rest, NT, preferred_element_type=jnp.float32)
            for chip in range(ny):
                r = 16 * chip
                msg[h, block, chip, 0:16, :] = main[r : r + 16, 0:128].astype(msg.dtype)
                msg[h, block, chip, 16:32, :] = main[r : r + 16, 128:256].astype(msg.dtype)
                tail = jnp.where(lane8 < 64, rest[r : r + 8], rest[r + 8 : r + 16])
                tail = jnp.concatenate([tail, blank], 0)
                msg[h, block, chip, 32:48, :] = tail.astype(msg.dtype)
            target = home(block, y)
            for i in range(ny):
                chip = lax.rem(y + i, ny)
                out.go(
                    msg.at[h, block, chip],
                    rcv.at[h, odd, z],
                    m_sem.at[h, odd, z],
                    {"prefix": 2 * chip + c, "sample": target},
                    None if i > 0 else target != z,
                )

            @pl.when(target == z)
            def _():
                rcv[h, odd, z] = msg[h, block, y]

    def collect(h):
        sums = []
        for k in range(2):
            chip = first_chip + k
            for i in range(nz):
                zz = lax.rem(z + i, nz)
                if i > 0:
                    arrived(rcv.at[h, k, zz], m_sem.at[h, k, zz])
                else:

                    @pl.when(chip != y)
                    def _():
                        arrived(rcv.at[h, k, zz], m_sem.at[h, k, zz])

        for k in range(2):
            total = rcv[h, k, 0].astype(jnp.float32)
            for zz in range(1, nz):
                total = total + rcv[h, k, zz].astype(jnp.float32)
            sums.append(total)
        a, d = sums
        at = slice(16 * h, 16 * h + 16)
        out_ref[at, 0:128] = a[0:16].astype(out_ref.dtype)
        out_ref[at, 128:256] = a[16:32].astype(out_ref.dtype)
        u, e = a[32:40], d[32:40]
        low = jnp.where(lane8 < 64, u, pltpu.roll(e, 64, 1))
        high = jnp.where(lane8 < 64, pltpu.roll(u, 64, 1), e)
        out_ref[at, 256:384] = jnp.concatenate([low, high], 0).astype(out_ref.dtype)
        out_ref[at, 384:512] = d[0:16].astype(out_ref.dtype)
        out_ref[at, 512:640] = d[16:32].astype(out_ref.dtype)

    attend_b(0)
    attend_b(1)
    merge(0)
    arrived(obuf.at[x, orow], loc.at[7])
    for which, source in enumerate(x_sources + [x]):
        arrived(obuf.at[source, orow_t], ot_sem.at[which])
    merge(1)
    output(0)
    output(1)
    collect(0)
    collect(1)
    out.finish()


def block_of(px, ny, nz, lengths, windows, hid, wq, wk, wv, wo, qg, kg, keys, values, gk, gv):
    nn = 2 * ny
    rows = hid.shape[0]
    batch = rows // 8
    half = batch // 2
    depth = wq.shape[0]
    qcols = wq.shape[1]
    cols = qcols + 2 * wk.shape[1]
    cut = qcols // 2
    heads = qcols // 128
    gr = 4 * heads
    window = 2 * depth + 64
    any_spec = pl.BlockSpec(memory_space=pl.ANY)
    vmem = pl.BlockSpec(memory_space=pltpu.VMEM)
    smem = pl.BlockSpec(memory_space=pltpu.SMEM)
    dma = pltpu.SemaphoreType.DMA
    bf = jnp.bfloat16
    f32 = jnp.float32
    scratch = [
        (keys.shape, bf),
        (values.shape, bf),
        (gk.shape, bf),
        (gv.shape, bf),
        ((px, window, cols), bf),
        ((px, 2 * depth, wo.shape[1]), bf),
        ((ny, px, rows, window), bf),
        ((ny * rows, cols), f32),
        ((ny, rows, cut), bf),
        ((ny, rows, cols - cut), bf),
        ((ny, rows, cut), bf),
        ((ny, rows, cols - cut), bf),
        ((batch, gr, 128), f32),
        ((nn, batch, gr, 128), bf),
        ((nn, batch, gr, 128), bf),
        ((batch, 16, 128), bf),
        ((batch, 16, 128), bf),
        ((nn, batch, gr, 128), bf),
        ((nn, batch, gr, 128), bf),
        ((8, nn * gr), f32),
        ((2, 8, nn * gr), f32),
        ((nn, batch, gr, 128), bf),
        ((nn, 2, half, gr, 128), bf),
        ((nn, 8, nn * gr), f32),
        ((nn, 2, 8, nn * gr), f32),
        ((batch, 2 * gr, 128), f32),
        ((2, 8, 128), f32),
        ((16, qcols), f32),
        ((2, ny, 16, qcols), bf),
        ((2, px, ny, 48, 128), bf),
        ((2, 2, nz, 48, 128), bf),
    ]
    return pl.pallas_call(
        functools.partial(kernel, px, ny, nz),
        out_shape=jax.ShapeDtypeStruct((rows, 640), bf),
        in_specs=[smem, smem] + [any_spec] * 5 + [vmem] * 2 + [any_spec] * 4,
        out_specs=vmem,
        scratch_shapes=[pltpu.VMEM(shape, dtype) for shape, dtype in scratch]
        + [
            dma((160,)),
            dma((8,)),
            dma((2, 3)),
            dma((2, 4)),
            dma((ny,)),
            dma((2, ny)),
            dma((2, nn)),
            dma((3,)),
            dma((4,)),
            dma((3, nn)),
            dma((3, nn)),
            dma((2, ny)),
            dma((2, 2, nz)),
        ],
        compiler_params=pltpu.CompilerParams(
            collective_id=0, has_side_effects=True, vmem_limit_bytes=60 * 2**20
        ),
        name="block",
    )(lengths, windows, hid, wq, wk, wv, wo, qg, kg, keys, values, gk, gv)


def on_device(
    px, ny, nz,
    new_hidden, query_projection_weight, key_projection_weight, value_projection_weight, w_out,
    query_norm_gain, key_norm_gain, prefix_keys, prompt_cache_values,
    generated_keys, generated_values, prompt_lengths, window_lengths,
):
    batch, samples, steps, width = new_hidden.shape
    dim = query_norm_gain.shape[0]
    block = block_of(
        px,
        ny,
        nz,
        prompt_lengths,
        window_lengths.T,
        new_hidden.reshape(batch * samples * steps, width),
        query_projection_weight,
        key_projection_weight,
        value_projection_weight,
        w_out.T,
        query_norm_gain.reshape(1, dim),
        key_norm_gain.reshape(1, dim),
        prefix_keys.reshape(batch, -1, dim),
        prompt_cache_values.reshape(batch, -1, dim),
        generated_keys.reshape(batch, -1, dim),
        generated_values.reshape(batch, -1, dim),
    )
    return block.reshape(batch, samples, steps, -1)


def solution(mesh):
    sizes = mesh.shape
    body = functools.partial(
        on_device, sizes["prompt"], sizes["prefix"] // 2, sizes["sample"]
    )
    return jax.shard_map(
        body,
        mesh=mesh,
        in_specs=(
            P("prompt", "prefix", None, None),
            P(("prompt", "prefix"), "sample"),
            P(("prompt", "prefix"), "sample"),
            P(("prompt", "prefix"), "sample"),
            P("sample", ("prompt", "prefix")),
            P(),
            P(),
            P("prompt", "prefix", "sample", None),
            P("prompt", "prefix", "sample", None),
            P("prompt", "prefix", None, "sample", None),
            P("prompt", "prefix", None, "sample", None),
            P("prompt"),
            P("prompt", "prefix"),
        ),
        out_specs=P("prompt", "prefix", None, "sample"),
        check_vma=False,
    )
```

time: 400 us -> 87.1 us (0.22)
  waiting for transfers between devices: 209 us -> 0 us
  blocking collectives: 98.4 us -> 0 us
  Pallas kernels: 0 us -> 83.6 us
  matrix products: 40.8 us -> 0 us
  other arithmetic: 19.3 us -> 0 us
  between operations: 14 us -> 0.01 us
  local copies, waits for them, and re-layouts: 15.6 us -> 3.17 us
    reduce_scatter x1 -> x0, waiting for transfers between devices: 86.8 us -> none  [on_device(): lax.psum_scatter(jnp.dot(spread, weights, preferred_element_type=jnp.floa...]
    pallas_call x0 -> x1, Pallas kernels: none -> 83.6 us  [block_of(): pl.pallas_call(functools.partial(kernel, px, ny, nz), out_shape=jax.Shape...]
    unnamed x6 -> x0, waiting for transfers between devices: 73.8 us -> none
    all_gather x1 -> x0, waiting for transfers between devices: 48.8 us -> none  [on_device(): lax.all_gather(attended, ('prompt', 'prefix'), axis=0, tiled=True)]
    dot_general x8 -> x0, matrix products: 40.8 us -> none  [the longest x1 15.9 us: on_device(): jnp.einsum('psrhgn,pnhd->psrhgd', weight.astype(jnp.bfloat16), prompt_cac...]
    all_to_all x2 -> x0, blocking collectives: 34.4 us -> none  [the longest x1 18.3 us: on_device(): lax.all_to_all(token_matrix, ('prompt', 'prefix'), split_axis=1, concat_a...]
    pmax x1 -> x0, blocking collectives: 27 us -> none  [on_device(): global_top = lax.pmax(local_top, 'prefix')]
    unnamed x1 -> x0, blocking collectives: 23.9 us -> none
  transfers between devices with their start and end apart: 4 -> 0, of which waited for: 4 -> 0; matrix products, arithmetic and copies ran while one was open for 2% -> 0% of each run, Pallas kernels for 0% -> 0%
where the time goes in v2:
time: 87.1 us; the launch traced here: 86.8 us
  Pallas kernels  83.6 us (96%)
  local copies, waits for them, and re-layouts  3.17 us (4%)
    pallas_call x1, Pallas kernels, block_of(): pl.pallas_call(functools.partial(kernel, px, ny, nz), out_shape=jax.Shape...  83.6 us
    reshape x1, local copies, waits for them, and re-layouts, on_device(): new_hidden.reshape(batch * samples * steps, width)  1.76 us

profile of v2, /device:TPU:32, one launch (start us, length us, event | category | flops | bytes accessed | tf_op | source)
XLA Modules:
  0.0 86.8 jit_solution(6205412537476184606)
XLA Ops:
  0.0 1.8 %reshape.24.hid = bf16[32,5120]{1,0:T(8,128)(2,1)} reshape(bf16[4,2,4,5120]{3,2,1,0:T(4,128)(2,1)} %param.13) | data formatting | bytes 655360 | tf_op jit(solution)/shard_map/reshape | solution.py:586
  1.8 83.6 %block.1 = bf16[32,640]{1,0:T(8,128)(2,1)} custom-call(s32[4]{0:T(128)} %lengths.1, s32[2,4]{1,0:T(2,128)} %bitcast.13, bf16[32,5120]{1,0:T(8,128)(2,1)} %reshape.24.hid, bf16[160,1024]{1,0:T(8,128)(2,1)} %wq.1, bf16[160,128]{1,0:T(8,128)(2,1)} %wk.1, bf16[160,128]{1,0:T(8,128)(2,1)} %wv.1, bf16[160,1024]{1,0:T(8,128)(2,1)} %bitcast.12, ...), custom_call_target="tpu_custom_call" | custom-call | tf_op jit(solution)/shard_map/block/pallas_call | solution.py:544
  85.4 1.4 %reshape.31 = bf16[4,2,4,640]{3,2,1,0:T(4,128)(2,1)} reshape(bf16[32,640]{1,0:T(8,128)(2,1)} %block.1) | data formatting | bytes 81920 | tf_op jit(solution)/shard_map/reshape | solution.py:598

commit v3 on v2

--- a/solution.py
+++ b/solution.py
@@ -76,6 +76,9 @@
     odd = lax.rem(y, 2)
     right, left = lax.rem(x + 1, px), lax.rem(x + px - 1, px)
     across = lax.rem(x + 2, px)
+    xodd = lax.rem(x, 2)
+    partner = lax.rem(x + 1 + xodd * (px - 2), px)
+    other = lax.rem(x + px - 1 - xodd * (px - 2), px)
     rows, width = hid.shape
     batch = keys.shape[0]
     keys_here = keys.shape[1]
@@ -89,10 +92,10 @@
     heads = qcols // 128
     hh = heads // 2
     gr = 8 * hh
-    rate = LOG2E / math.sqrt(128)
     twin = {"prefix": 2 * y + 1 - c}
     peers = [lax.rem(y + i, ny) for i in range(1, ny)]
     others = [{"prefix": 2 * peer + c} for peer in peers]
+    beyond = [{"prompt": other, "prefix": 2 * chip + c} for chip in [y] + peers]
     prefix_peers = [lax.rem(n + i, nn) for i in range(1, nn)]
     x_targets = [{"prompt": right}, {"prompt": left}, {"prompt": across}]
     x_sources = [left, right, across]
@@ -107,12 +110,12 @@
         ((keys, kbuf), (values, vbuf), (gkeys, gkb), (gvalues, gvb))
     ):
         pltpu.make_async_copy(src, dst, loc.at[3 + i]).start()
-    zero = jnp.zeros((px, pad, cols), wbuf.dtype)
+    zero = jnp.zeros((2, pad, cols), wbuf.dtype)
     wbuf[:, 0:pad, :] = zero
     wbuf[:, pair : pair + pad, :] = zero
 
     barrier = pltpu.get_barrier_semaphore()
-    greeted = x_targets + [{"prefix": peer} for peer in prefix_peers]
+    greeted = x_targets + [{"prefix": peer} for peer in prefix_peers] + beyond[1:]
     for device in greeted:
         pl.semaphore_signal(barrier, inc=1, device_id=device, device_id_type=MESH)
     for k in range(2):
@@ -145,82 +148,78 @@
     )
     spans = (slice(0, cut), slice(cut, cols))
 
-    def send_weights(group, which):
+    def send_weights(group):
         for piece, lo, size in (group_a, group_b)[group]:
-            spot = wbuf.at[x, mine, lo : lo + size]
-            if which == 3:
-                out.go(piece, spot, tw_sem.at[group, 3], twin)
-            elif which == 4:
-                pltpu.make_async_copy(piece, spot, loc.at[group]).start()
-            else:
-                out.go(piece, spot, w_sem.at[group, which], x_targets[which])
+            spot = wbuf.at[1, mine, lo : lo + size]
+            out.go(piece, spot, w_sem.at[group], {"prompt": partner})
+        for piece, lo, size in (group_a, group_b)[group]:
+            spot = wbuf.at[0, mine, lo : lo + size]
+            out.go(piece, spot, tw_sem.at[group, 0], twin)
+            pltpu.make_async_copy(piece, spot, loc.at[group]).start()
 
     def start_of(block, chip):
         return pl.multiple_of(128 * lax.div(pair * ny * block + pair * chip, 128), 128)
 
-    for which in range(3):
-        send_weights(0, which)
-    for peer, device in zip(peers, others):
-        for block in range(px):
-            out.go(
-                hid.at[:, pl.ds(start_of(block, peer), window)],
-                tok.at[y, block],
-                t_sem.at[y],
-                device,
-            )
-    send_weights(0, 3)
-    send_weights(0, 4)
-    for block in range(px):
-        pltpu.make_async_copy(
-            hid.at[:, pl.ds(start_of(block, y), window)], tok.at[y, block], loc.at[2]
-        ).start()
-    send_weights(1, 3)
-    send_weights(1, 4)
-
-    def multiply(block, group, start):
-        span = spans[group]
-        lhs = tok[:, block].reshape(ny * rows, window)
-        value = jnp.dot(lhs, wbuf[block, :, span], preferred_element_type=jnp.float32)
-        if start:
-            acc[:, span] = value
-        else:
-            acc[:, span] += value
+    send_weights(0)
+    blocks = ((x, partner), (other, lax.rem(other + 1 + (1 - xodd) * (px - 2), px)))
+    for i in range(2):
+        for chip, device in zip([y] + peers, ([None] + others, beyond)[i]):
+            for j in range(2):
+                piece = hid.at[:, pl.ds(start_of(blocks[i][j], chip), window)]
+                spot = tok.at[j, i, y]
+                if device is None:
+                    pltpu.make_async_copy(piece, spot, loc.at[8 + j]).start()
+                else:
+                    out.go(piece, spot, t_sem.at[j, i, y], device)
+
+    def multiply(block, group):
+        lhs = tok[block].reshape(2 * ny * rows, window)
+        return jnp.dot(
+            lhs, wbuf[block, :, spans[group]], preferred_element_type=jnp.float32
+        )
 
     orow = pl.ds(pl.multiple_of(depth * c, 16), depth)
     orow_t = pl.ds(pl.multiple_of(depth * (1 - c), 16), depth)
 
+    def tokens_of(block):
+        arrived(tok.at[block, 0, y], loc.at[8 + block])
+        for peer in peers:
+            arrived(tok.at[block, 0, peer], t_sem.at[block, 0, peer])
+        for chip in [y] + peers:
+            arrived(tok.at[block, 1, chip], t_sem.at[block, 1, chip])
+
     def project(group, after):
         span = spans[group]
-        arrived(wbuf.at[x, mine, span], loc.at[group])
+        arrived(wbuf.at[1, mine, span], w_sem.at[group])
+        out.go(wbuf.at[1, mine, span], wbuf.at[1, mine, span], tw_sem.at[group, 1], twin)
+        after()
+        arrived(wbuf.at[0, mine, span], loc.at[group])
+        arrived(wbuf.at[0, theirs, span], tw_sem.at[group, 0])
         if group == 0:
-            arrived(tok.at[y], loc.at[2])
-            for peer in peers:
-                arrived(tok.at[peer], t_sem.at[peer])
-        arrived(wbuf.at[x, theirs, span], tw_sem.at[group, 3])
-        multiply(x, group, True)
-        for which, source in enumerate(x_sources):
-            spot = wbuf.at[source, mine, span]
-            arrived(spot, w_sem.at[group, which])
-            out.go(spot, spot, tw_sem.at[group, which], twin)
-            after(which)
-        for which, source in enumerate(x_sources):
-            arrived(wbuf.at[source, theirs, span], tw_sem.at[group, which])
-            multiply(source, group, False)
+            tokens_of(0)
+            tokens_of(1)
+        acc[:, span] = multiply(0, group)
+        arrived(wbuf.at[1, theirs, span], tw_sem.at[group, 1])
         part, red = ((part_a, red_a), (part_b, red_b))[group]
-        part[...] = acc[:, span].astype(part.dtype).reshape(part.shape)
+        sums = acc[:, span] + multiply(1, group)
+        part[...] = sums.astype(part.dtype).reshape(part.shape)
         for peer, device in zip(peers, others):
-            out.go(part.at[peer], red.at[y], r_sem.at[group, y], device)
-        red[y] = part[y]
-
-    gain = qg[...].astype(jnp.float32)
+            out.go(part.at[0, peer], red.at[0, y], r_sem.at[group, 0, y], device)
+        for chip, device in zip([y] + peers, beyond):
+            out.go(part.at[1, chip], red.at[1, y], r_sem.at[group, 1, y], device)
+        red[0, y] = part[0, y]
+
+    gain = qg[...].astype(jnp.float32) * (LOG2E / math.sqrt(128))
 
     def own(group):
         red = (red_a, red_b)[group]
         for peer in peers:
-            arrived(red.at[peer], r_sem.at[group, peer])
-        total = red[0].astype(jnp.float32)
-        for chip in range(1, ny):
-            total = total + red[chip].astype(jnp.float32)
+            arrived(red.at[0, peer], r_sem.at[group, 0, peer])
+        for chip in [y] + peers:
+            arrived(red.at[1, chip], r_sem.at[group, 1, chip])
+        total = red[0, 0].astype(jnp.float32)
+        for i in range(1, 2 * ny):
+            total = total + red[i // ny, i % ny].astype(jnp.float32)
         for head in range(hh):
             value = norm(total[:, 128 * head : 128 * head + 128], gain)
             for b in range(batch):
@@ -236,33 +235,34 @@
         for peer in prefix_peers:
             arrived(q.at[peer], q_sem.at[group, peer])
 
-    def attend(b, group, store_lse):
-        q = (qa, qb)[group][:, b].reshape(nn * gr, 128)
-        valid = lengths[b] - n * keys_here
-        top = total = value = None
-        for lo in range(0, keys_here, CHUNK):
-            size = min(CHUNK, keys_here - lo)
-            k = kbuf[b, lo : lo + size]
-            v = vbuf[b, lo : lo + size]
-            s = lax.dot_general(k, q, NT, preferred_element_type=jnp.float32)
-            at = lo + lax.broadcasted_iota(jnp.int32, (size, 1), 0)
-            s = s + jnp.where(at < valid, 0.0, -1e30)
-            here = jnp.max(s, axis=0, keepdims=True)
-            new = here if top is None else jnp.maximum(top, here)
-            w = jnp.exp2((s - new) * rate)
-            add = jnp.sum(w, axis=0, keepdims=True)
-            val = lax.dot_general(
-                v, w.astype(jnp.bfloat16), TN, preferred_element_type=jnp.float32
-            )
-            if top is None:
-                total, value = add, val
-            else:
-                factor = jnp.exp2((top - new) * rate)
-                total, value = total * factor + add, value * factor + val
-            top = new
-        p = (pa, pb)[group]
-        p[:, b] = (value / total).T.astype(p.dtype).reshape(nn, gr, 128)
-        store_lse(top * rate + jnp.log2(total))
+    def attend(h, group, store_lse):
+        for i in range(half):
+            b = half * h + i
+            q = (qa, qb)[group][:, b].reshape(nn * gr, 128)
+            valid = lengths[b] - n * keys_here
+            top = total = value = None
+            scores = []
+            for lo in range(0, keys_here, CHUNK):
+                size = min(CHUNK, keys_here - lo)
+                k = kbuf[b, lo : lo + size]
+                s = lax.dot_general(k, q, NT, preferred_element_type=jnp.float32)
+                at = lo + lax.broadcasted_iota(jnp.int32, (size, 1), 0)
+                s = s + jnp.where(at < valid, 0.0, -1e30)
+                here = jnp.max(s, axis=0, keepdims=True)
+                top = here if top is None else jnp.maximum(top, here)
+                scores.append(s)
+            for s, lo in zip(scores, range(0, keys_here, CHUNK)):
+                w = jnp.exp2(s - top)
+                add = jnp.sum(w, axis=0, keepdims=True)
+                v = vbuf[b, lo : lo + s.shape[0]]
+                val = lax.dot_general(
+                    v, w.astype(jnp.bfloat16), TN, preferred_element_type=jnp.float32
+                )
+                total = add if total is None else total + add
+                value = val if value is None else value + val
+            p = (pa, pb)[group]
+            p[:, b] = (value / total).T.astype(p.dtype).reshape(nn, gr, 128)
+            store_lse(i, top + jnp.log2(total))
 
     def attend_own(b):
         q = jnp.concatenate([qa[n, b], qb[n, b]], 0)
@@ -280,42 +280,31 @@
         top = jnp.maximum(
             jnp.max(s1, axis=-1, keepdims=True), jnp.max(s2, axis=-1, keepdims=True)
         )
-        w1 = jnp.exp2((s1 - top) * rate)
-        w2 = jnp.exp2((s2 - top) * rate)
+        w1 = jnp.exp2(s1 - top)
+        w2 = jnp.exp2(s2 - top)
         total = jnp.sum(w1, axis=-1, keepdims=True) + jnp.sum(w2, axis=-1, keepdims=True)
         value = jnp.dot(w1.astype(jnp.bfloat16), gvb[b], preferred_element_type=jnp.float32)
         value = value + jnp.dot(
             w2.astype(jnp.bfloat16), vn[b], preferred_element_type=jnp.float32
         )
         ow[b] = value / total
-        lse = top * rate + jnp.log2(total)
+        lse = top + jnp.log2(total)
         lw[0, pl.ds(b, 1), :] = lanes_of(lse[0:gr], gr)
         lw[1, pl.ds(b, 1), :] = lanes_of(lse[gr:], gr)
 
-    project(0, lambda which: send_weights(1, which))
+    half = batch // 2
+    project(0, lambda: send_weights(1))
+
+    def send_wo():
+        for which in range(3):
+            out.go(wo, obuf.at[x, orow], o_sem.at[which], x_targets[which])
+        out.go(wo, obuf.at[x, orow], ot_sem.at[3], twin)
+        pltpu.make_async_copy(wo, obuf.at[x, orow], loc.at[7]).start()
+
+    project(1, lambda: None)
     own(0)
-
-    def send_wo(which):
-        out.go(wo, obuf.at[x, orow], o_sem.at[which], x_targets[which])
-
-    project(1, send_wo)
-    out.go(wo, obuf.at[x, orow], ot_sem.at[3], twin)
-    pltpu.make_async_copy(wo, obuf.at[x, orow], loc.at[7]).start()
-
-    arrived(kbuf, loc.at[3])
-    arrived(vbuf, loc.at[4])
-    queries(0)
-
-    def attend_a(b, _):
-        def store(lse):
-            la[pl.ds(b, 1), :] = lse
-
-        attend(b, 0, store)
-        return 0
-
-    lax.fori_loop(0, batch // 2, attend_a, 0)
-
     total = own(1)
+    send_wo()
     q_there = qcols - cut
     k_new = norm(total[:, q_there : q_there + kcols], kg[...].astype(jnp.float32))
     v_new = total[:, q_there + kcols :]
@@ -324,39 +313,26 @@
         kn[b] = jnp.concatenate([k_new[8 * b : 8 * b + 8], blank], 0).astype(kn.dtype)
         vn[b] = jnp.concatenate([v_new[8 * b : 8 * b + 8], blank], 0).astype(vn.dtype)
 
-    lax.fori_loop(batch // 2, batch, attend_a, 0)
+    arrived(kbuf, loc.at[3])
+    arrived(vbuf, loc.at[4])
+    queries(0)
+    for h in range(2):
+
+        def store_a(i, lse):
+            la[half * h + i : half * h + i + 1, :] = lse
+
+        attend(h, 0, store_a)
     for peer in prefix_peers:
         out.go(la, sa.at[n], s_sem.at[0, n], {"prefix": peer})
         out.go(pa.at[peer], ra.at[n], p_sem.at[0, n], {"prefix": peer})
     ra[n] = pa[n]
     sa[n] = la[...]
 
-    arrived(gkb, loc.at[5])
-    arrived(gvb, loc.at[6])
-
-    def own_body(b, _):
-        attend_own(b)
-        return 0
-
-    lax.fori_loop(0, batch, own_body, 0)
-
-    for which, source in enumerate(x_sources):
-        spot = obuf.at[source, orow]
-        arrived(spot, o_sem.at[which])
-        out.go(spot, spot, ot_sem.at[which], twin)
-
-    queries(1)
-    half = batch // 2
-
     def attend_b(h):
-        def body(i, _):
-            def store(lse):
-                lb[h, pl.ds(i, 1), :] = lse
-
-            attend(h * half + i, 1, store)
-            return 0
-
-        lax.fori_loop(0, half, body, 0)
+        def store_b(i, lse):
+            lb[h, i : i + 1, :] = lse
+
+        attend(h, 1, store_b)
         span = slice(h * half, h * half + half)
         for peer in prefix_peers:
             device = {"prefix": peer}
@@ -476,9 +452,23 @@
         out_ref[at, 384:512] = d[0:16].astype(out_ref.dtype)
         out_ref[at, 512:640] = d[16:32].astype(out_ref.dtype)
 
+    queries(1)
     attend_b(0)
+
     attend_b(1)
+    arrived(gkb, loc.at[5])
+    arrived(gvb, loc.at[6])
+
+    def own_body(b, _):
+        attend_own(b)
+        return 0
+
+    lax.fori_loop(0, batch, own_body, 0)
     merge(0)
+    for which, source in enumerate(x_sources):
+        spot = obuf.at[source, orow]
+        arrived(spot, o_sem.at[which])
+        out.go(spot, spot, ot_sem.at[which], twin)
     arrived(obuf.at[x, orow], loc.at[7])
     for which, source in enumerate(x_sources + [x]):
         arrived(obuf.at[source, orow_t], ot_sem.at[which])
@@ -513,14 +503,14 @@
         (values.shape, bf),
         (gk.shape, bf),
         (gv.shape, bf),
-        ((px, window, cols), bf),
+        ((2, window, cols), bf),
         ((px, 2 * depth, wo.shape[1]), bf),
-        ((ny, px, rows, window), bf),
-        ((ny * rows, cols), f32),
-        ((ny, rows, cut), bf),
-        ((ny, rows, cols - cut), bf),
-        ((ny, rows, cut), bf),
-        ((ny, rows, cols - cut), bf),
+        ((2, 2, ny, rows, window), bf),
+        ((2 * ny * rows, cols), f32),
+        ((2, ny, rows, cut), bf),
+        ((2, ny, rows, cols - cut), bf),
+        ((2, ny, rows, cut), bf),
+        ((2, ny, rows, cols - cut), bf),
         ((batch, gr, 128), f32),
         ((nn, batch, gr, 128), bf),
         ((nn, batch, gr, 128), bf),
@@ -548,12 +538,12 @@
         out_specs=vmem,
         scratch_shapes=[pltpu.VMEM(shape, dtype) for shape, dtype in scratch]
         + [
-            dma((160,)),
-            dma((8,)),
-            dma((2, 3)),
-            dma((2, 4)),
-            dma((ny,)),
-            dma((2, ny)),
+            dma((144,)),
+            dma((10,)),
+            dma((2,)),
+            dma((2, 2)),
+            dma((2, 2, ny)),
+            dma((2, 2, ny)),
             dma((2, nn)),
             dma((3,)),
             dma((4,)),

time: 87.1 us -> 76.8 us (0.88)
  Pallas kernels: 83.6 us -> 73.4 us
    pallas_call x1, Pallas kernels: 83.6 us -> 73.4 us  [block_of(): pl.pallas_call(functools.partial(kernel, px, ny, nz), out_shape=jax.Shape...]
where the time goes in v3:
time: 76.8 us; the launch traced here: 76.6 us
  Pallas kernels  73.4 us (96%)
  local copies, waits for them, and re-layouts  3.17 us (4%)
    pallas_call x1, Pallas kernels, block_of(): pl.pallas_call(functools.partial(kernel, px, ny, nz), out_shape=jax.Shape...  73.4 us
    reshape x1, local copies, waits for them, and re-layouts, on_device(): new_hidden.reshape(batch * samples * steps, width)  1.76 us

profile of v3, /device:TPU:32, one launch (start us, length us, event | category | flops | bytes accessed | tf_op | source)
XLA Modules:
  0.0 76.6 jit_solution(1276249006543299312)
XLA Ops:
  0.0 1.8 %reshape.24.hid = bf16[32,5120]{1,0:T(8,128)(2,1)} reshape(bf16[4,2,4,5120]{3,2,1,0:T(4,128)(2,1)} %param.13) | data formatting | bytes 655360 | tf_op jit(solution)/shard_map/reshape | solution.py:576
  1.8 73.4 %block.1 = bf16[32,640]{1,0:T(8,128)(2,1)} custom-call(s32[4]{0:T(128)} %lengths.1, s32[2,4]{1,0:T(2,128)} %bitcast.13, bf16[32,5120]{1,0:T(8,128)(2,1)} %reshape.24.hid, bf16[160,1024]{1,0:T(8,128)(2,1)} %wq.1, bf16[160,128]{1,0:T(8,128)(2,1)} %wk.1, bf16[160,128]{1,0:T(8,128)(2,1)} %wv.1, bf16[160,1024]{1,0:T(8,128)(2,1)} %bitcast.12, ...), custom_call_target="tpu_custom_call" | custom-call | tf_op jit(solution)/shard_map/block/pallas_call | solution.py:534
  75.2 1.4 %reshape.31 = bf16[4,2,4,640]{3,2,1,0:T(4,128)(2,1)} reshape(bf16[32,640]{1,0:T(8,128)(2,1)} %block.1) | data formatting | bytes 81920 | tf_op jit(solution)/shard_map/reshape | solution.py:588

commit v4 on v3

--- a/solution.py
+++ b/solution.py
@@ -16,15 +16,24 @@
 
 
 class Sends:
-    def __init__(self, sems):
-        self.sems = sems
-        self.started = []
+    def __init__(self, sems, single, ruler):
+        self.sems, self.single, self.ruler = sems, single, ruler
+        self.totals = [0]
+        self.conditional = []
 
     def go(self, src, dst, recv, device, when=None):
+        if when is None:
+            size = math.prod(src.shape) * src.dtype.itemsize // 256
+            if self.totals[-1] + size > self.ruler.shape[0]:
+                self.totals.append(0)
+            self.totals[-1] += size
+            sem = self.sems.at[len(self.totals) - 1]
+        else:
+            sem = self.single.at[len(self.conditional)]
         copy = pltpu.make_async_remote_copy(
             src_ref=src,
             dst_ref=dst,
-            send_sem=self.sems.at[len(self.started)],
+            send_sem=sem,
             recv_sem=recv,
             device_id=device,
             device_id_type=MESH,
@@ -33,14 +42,13 @@
             copy.start()
         else:
             pl.when(when)(copy.start)
-        self.started.append((copy, when))
+            self.conditional.append((copy, when))
 
     def finish(self):
-        for copy, when in self.started:
-            if when is None:
-                copy.wait_send()
-            else:
-                pl.when(when)(copy.wait_send)
+        for i, total in enumerate(self.totals):
+            arrived(self.ruler.at[0:total], self.sems.at[i])
+        for copy, when in self.conditional:
+            pl.when(when)(copy.wait_send)
 
 
 def arrived(ref, sem):
@@ -65,8 +73,8 @@
     lengths, windows, hid, wq, wk, wv, wo, qg, kg, keys, values, gkeys, gvalues,
     out_ref,
     kbuf, vbuf, gkb, gvb, wbuf, obuf, tok, acc, part_a, part_b, red_a, red_b,
-    qf, qa, qb, kn, vn, pa, pb, la, lb, ra, rb, sa, sb, ow, lw, attf, att, msg, rcv,
-    send, loc, w_sem, tw_sem, t_sem, r_sem, q_sem, o_sem, ot_sem, p_sem, s_sem, a_sem, m_sem,
+    qf, qa, qb, kn, vn, pa, pb, la, lb, ra, rb, sa, sb, ow, lw, attf, att, msg, rcv, ruler,
+    send, single, loc, w_sem, tw_sem, t_sem, r_sem, q_sem, o_sem, ot_sem, p_sem, s_sem, a_sem, m_sem,
 ):
     nn = 2 * ny
     x = lax.axis_index("prompt")
@@ -136,7 +144,7 @@
         mine_too = mine_too + (home(block, y) == z).astype(jnp.int32)
     pl.semaphore_wait(barrier, len(greeted) + px * ny - mine_too)
 
-    out = Sends(send)
+    out = Sends(send, single, ruler)
     base = pl.multiple_of(pad * odd + depth * c, 16)
     mine = pl.ds(base, depth)
     theirs = pl.ds(pl.multiple_of(pad * odd + depth * (1 - c), 16), depth)
@@ -168,9 +176,9 @@
                 piece = hid.at[:, pl.ds(start_of(blocks[i][j], chip), window)]
                 spot = tok.at[j, i, y]
                 if device is None:
-                    pltpu.make_async_copy(piece, spot, loc.at[8 + j]).start()
+                    pltpu.make_async_copy(piece, spot, t_sem.at[0]).start()
                 else:
-                    out.go(piece, spot, t_sem.at[j, i, y], device)
+                    out.go(piece, spot, t_sem.at[0], device)
 
     def multiply(block, group):
         lhs = tok[block].reshape(2 * ny * rows, window)
@@ -180,13 +188,6 @@
 
     orow = pl.ds(pl.multiple_of(depth * c, 16), depth)
     orow_t = pl.ds(pl.multiple_of(depth * (1 - c), 16), depth)
-
-    def tokens_of(block):
-        arrived(tok.at[block, 0, y], loc.at[8 + block])
-        for peer in peers:
-            arrived(tok.at[block, 0, peer], t_sem.at[block, 0, peer])
-        for chip in [y] + peers:
-            arrived(tok.at[block, 1, chip], t_sem.at[block, 1, chip])
 
     def project(group, after):
         span = spans[group]
@@ -196,44 +197,41 @@
         arrived(wbuf.at[0, mine, span], loc.at[group])
         arrived(wbuf.at[0, theirs, span], tw_sem.at[group, 0])
         if group == 0:
-            tokens_of(0)
-            tokens_of(1)
+            arrived(tok, t_sem.at[0])
         acc[:, span] = multiply(0, group)
         arrived(wbuf.at[1, theirs, span], tw_sem.at[group, 1])
         part, red = ((part_a, red_a), (part_b, red_b))[group]
         sums = acc[:, span] + multiply(1, group)
         part[...] = sums.astype(part.dtype).reshape(part.shape)
         for peer, device in zip(peers, others):
-            out.go(part.at[0, peer], red.at[0, y], r_sem.at[group, 0, y], device)
+            out.go(part.at[0, peer], red.at[y], r_sem.at[group], device)
         for chip, device in zip([y] + peers, beyond):
-            out.go(part.at[1, chip], red.at[1, y], r_sem.at[group, 1, y], device)
-        red[0, y] = part[0, y]
-
-    gain = qg[...].astype(jnp.float32) * (LOG2E / math.sqrt(128))
+            out.go(part.at[1, chip], red.at[ny + y], r_sem.at[group], device)
+        red[y] = part[0, y]
+
+    def gain():
+        return qg[...].astype(jnp.float32) * (LOG2E / math.sqrt(128))
+
 
     def own(group):
         red = (red_a, red_b)[group]
-        for peer in peers:
-            arrived(red.at[0, peer], r_sem.at[group, 0, peer])
-        for chip in [y] + peers:
-            arrived(red.at[1, chip], r_sem.at[group, 1, chip])
-        total = red[0, 0].astype(jnp.float32)
-        for i in range(1, 2 * ny):
-            total = total + red[i // ny, i % ny].astype(jnp.float32)
+        arrived(red.at[0 : nn - 1], r_sem.at[group])
+        total = red[0].astype(jnp.float32)
+        for i in range(1, nn):
+            total = total + red[i].astype(jnp.float32)
         for head in range(hh):
-            value = norm(total[:, 128 * head : 128 * head + 128], gain)
+            value = norm(total[:, 128 * head : 128 * head + 128], gain())
             for b in range(batch):
                 qf[b, 8 * head : 8 * head + 8, :] = value[8 * b : 8 * b + 8]
         q = (qa, qb)[group]
         q[n] = qf[...].astype(q.dtype)
         for peer in prefix_peers:
-            out.go(q.at[n], q.at[n], q_sem.at[group, n], {"prefix": peer})
+            out.go(q.at[n], q.at[n], q_sem.at[group], {"prefix": peer})
         return total
 
     def queries(group):
         q = (qa, qb)[group]
-        for peer in prefix_peers:
-            arrived(q.at[peer], q_sem.at[group, peer])
+        arrived(q.at[0 : nn - 1], q_sem.at[group])
 
     def attend(h, group, store_lse):
         for i in range(half):
@@ -297,9 +295,9 @@
 
     def send_wo():
         for which in range(3):
-            out.go(wo, obuf.at[x, orow], o_sem.at[which], x_targets[which])
-        out.go(wo, obuf.at[x, orow], ot_sem.at[3], twin)
-        pltpu.make_async_copy(wo, obuf.at[x, orow], loc.at[7]).start()
+            out.go(wo, obuf.at[x, orow], o_sem.at[0], x_targets[which])
+        out.go(wo, obuf.at[x, orow], ot_sem.at[0], twin)
+        pltpu.make_async_copy(wo, obuf.at[x, orow], loc.at[2]).start()
 
     project(1, lambda: None)
     own(0)
@@ -323,8 +321,8 @@
 
         attend(h, 0, store_a)
     for peer in prefix_peers:
-        out.go(la, sa.at[n], s_sem.at[0, n], {"prefix": peer})
-        out.go(pa.at[peer], ra.at[n], p_sem.at[0, n], {"prefix": peer})
+        out.go(la, sa.at[n], s_sem.at[0], {"prefix": peer})
+        out.go(pa.at[peer], ra.at[n], p_sem.at[0], {"prefix": peer})
     ra[n] = pa[n]
     sa[n] = la[...]
 
@@ -336,8 +334,8 @@
         span = slice(h * half, h * half + half)
         for peer in prefix_peers:
             device = {"prefix": peer}
-            out.go(lb.at[h], sb.at[n, h], s_sem.at[1 + h, n], device)
-            out.go(pb.at[peer, span], rb.at[n, h], p_sem.at[1 + h, n], device)
+            out.go(lb.at[h], sb.at[n, h], s_sem.at[1 + h], device)
+            out.go(pb.at[peer, span], rb.at[n, h], p_sem.at[1 + h], device)
         rb[n, h] = pb[n, span]
         sb[n, h] = lb[h]
 
@@ -348,12 +346,10 @@
 
     def merge(h):
         if h == 0:
-            for peer in prefix_peers:
-                arrived(sa.at[peer], s_sem.at[0, peer])
-                arrived(ra.at[peer], p_sem.at[0, peer])
-        for peer in prefix_peers:
-            arrived(sb.at[peer, h], s_sem.at[1 + h, peer])
-            arrived(rb.at[peer, h], p_sem.at[1 + h, peer])
+            arrived(sa.at[0 : nn - 1], s_sem.at[0])
+            arrived(ra.at[0 : nn - 1], p_sem.at[0])
+        arrived(sb.at[0 : nn - 1, h], s_sem.at[1 + h])
+        arrived(rb.at[0 : nn - 1, h], p_sem.at[1 + h])
         shift = lax.rem(many - gr * n, many)
         for group in range(2):
             stats = []
@@ -385,13 +381,12 @@
                     attf[8 * i : 8 * i + 8, at : at + 128] = total[8 * head : 8 * head + 8]
         att[h, y] = attf[...].astype(att.dtype)
         for device in others:
-            out.go(att.at[h, y], att.at[h, y], a_sem.at[h, y], device)
+            out.go(att.at[h, y], att.at[h, y], a_sem.at[h], device)
 
     lane8 = lax.broadcasted_iota(jnp.int32, (8, 128), 1)
 
     def output(h):
-        for peer in peers:
-            arrived(att.at[h, peer], a_sem.at[h, peer])
+        arrived(att.at[h, 0 : ny - 1], a_sem.at[h])
         lhs = att[h].reshape(ny * 16, att.shape[3])
         blank = jnp.zeros((8, 128), jnp.float32)
         for block in range(px):
@@ -412,45 +407,43 @@
                 chip = lax.rem(y + i, ny)
                 out.go(
                     msg.at[h, block, chip],
-                    rcv.at[h, odd, z],
-                    m_sem.at[h, odd, z],
+                    rcv.at[h, odd * nz + z],
+                    m_sem.at[h],
                     {"prefix": 2 * chip + c, "sample": target},
                     None if i > 0 else target != z,
                 )
 
             @pl.when(target == z)
             def _():
-                rcv[h, odd, z] = msg[h, block, y]
+                rcv[h, odd * nz + z] = msg[h, block, y]
 
     def collect(h):
         sums = []
+        here = jnp.logical_or(first_chip == y, first_chip + 1 == y)
+
+        @pl.when(here)
+        def _():
+            arrived(rcv.at[h, 0 : 2 * nz - 1], m_sem.at[h])
+
+        @pl.when(jnp.logical_not(here))
+        def _():
+            arrived(rcv.at[h], m_sem.at[h])
+
         for k in range(2):
-            chip = first_chip + k
-            for i in range(nz):
-                zz = lax.rem(z + i, nz)
-                if i > 0:
-                    arrived(rcv.at[h, k, zz], m_sem.at[h, k, zz])
-                else:
-
-                    @pl.when(chip != y)
-                    def _():
-                        arrived(rcv.at[h, k, zz], m_sem.at[h, k, zz])
-
-        for k in range(2):
-            total = rcv[h, k, 0].astype(jnp.float32)
+            total = rcv[h, k * nz].astype(jnp.float32)
             for zz in range(1, nz):
-                total = total + rcv[h, k, zz].astype(jnp.float32)
+                total = total + rcv[h, k * nz + zz].astype(jnp.float32)
             sums.append(total)
         a, d = sums
-        at = slice(16 * h, 16 * h + 16)
-        out_ref[at, 0:128] = a[0:16].astype(out_ref.dtype)
-        out_ref[at, 128:256] = a[16:32].astype(out_ref.dtype)
         u, e = a[32:40], d[32:40]
         low = jnp.where(lane8 < 64, u, pltpu.roll(e, 64, 1))
         high = jnp.where(lane8 < 64, pltpu.roll(u, 64, 1), e)
-        out_ref[at, 256:384] = jnp.concatenate([low, high], 0).astype(out_ref.dtype)
-        out_ref[at, 384:512] = d[0:16].astype(out_ref.dtype)
-        out_ref[at, 512:640] = d[16:32].astype(out_ref.dtype)
+        middle = jnp.concatenate([low, high], 0)
+        tiles = (a[0:16], a[16:32], middle, d[0:16], d[16:32])
+        for j, tile in enumerate(tiles):
+            tile = tile.astype(out_ref.dtype)
+            for i in range(4):
+                out_ref[4 * h + i, :, 128 * j : 128 * j + 128] = tile[4 * i : 4 * i + 4]
 
     queries(1)
     attend_b(0)
@@ -465,13 +458,12 @@
 
     lax.fori_loop(0, batch, own_body, 0)
     merge(0)
-    for which, source in enumerate(x_sources):
+    arrived(obuf.at[0 : px - 1, orow], o_sem.at[0])
+    for source in x_sources:
         spot = obuf.at[source, orow]
-        arrived(spot, o_sem.at[which])
-        out.go(spot, spot, ot_sem.at[which], twin)
-    arrived(obuf.at[x, orow], loc.at[7])
-    for which, source in enumerate(x_sources + [x]):
-        arrived(obuf.at[source, orow_t], ot_sem.at[which])
+        out.go(spot, spot, ot_sem.at[0], twin)
+    arrived(obuf.at[x, orow], loc.at[2])
+    arrived(obuf.at[:, orow_t], ot_sem.at[0])
     merge(1)
     output(0)
     output(1)
@@ -509,8 +501,8 @@
         ((2 * ny * rows, cols), f32),
         ((2, ny, rows, cut), bf),
         ((2, ny, rows, cols - cut), bf),
-        ((2, ny, rows, cut), bf),
-        ((2, ny, rows, cols - cut), bf),
+        ((nn, rows, cut), bf),
+        ((nn, rows, cols - cut), bf),
         ((batch, gr, 128), f32),
         ((nn, batch, gr, 128), bf),
         ((nn, batch, gr, 128), bf),
@@ -529,28 +521,30 @@
         ((16, qcols), f32),
         ((2, ny, 16, qcols), bf),
         ((2, px, ny, 48, 128), bf),
-        ((2, 2, nz, 48, 128), bf),
+        ((2, 2 * nz, 48, 128), bf),
+        ((4096, 128), bf),
     ]
     return pl.pallas_call(
         functools.partial(kernel, px, ny, nz),
-        out_shape=jax.ShapeDtypeStruct((rows, 640), bf),
+        out_shape=jax.ShapeDtypeStruct((rows // 4, 4, 640), bf),
         in_specs=[smem, smem] + [any_spec] * 5 + [vmem] * 2 + [any_spec] * 4,
         out_specs=vmem,
         scratch_shapes=[pltpu.VMEM(shape, dtype) for shape, dtype in scratch]
         + [
-            dma((144,)),
             dma((10,)),
+            dma((2 * px,)),
+            dma((7,)),
             dma((2,)),
             dma((2, 2)),
-            dma((2, 2, ny)),
-            dma((2, 2, ny)),
-            dma((2, nn)),
+            dma((1,)),
+            dma((2,)),
+            dma((2,)),
+            dma((1,)),
+            dma((1,)),
             dma((3,)),
-            dma((4,)),
-            dma((3, nn)),
-            dma((3, nn)),
-            dma((2, ny)),
-            dma((2, 2, nz)),
+            dma((3,)),
+            dma((2,)),
+            dma((2,)),
         ],
         compiler_params=pltpu.CompilerParams(
             collective_id=0, has_side_effects=True, vmem_limit_bytes=60 * 2**20

time: 76.8 us -> 74.2 us (0.966)
  Pallas kernels: 73.4 us -> 70.8 us
    pallas_call x1, Pallas kernels: 73.4 us -> 70.8 us  [block_of(): pl.pallas_call(functools.partial(kernel, px, ny, nz), out_shape=jax.Shape...]
    unnamed x0 -> x1, local copies, waits for them, and re-layouts: none -> 1.41 us
    reshape x1 -> x0, local copies, waits for them, and re-layouts: 1.41 us -> none  [on_device(): return block.reshape(batch, samples, steps, -1)]
where the time goes in v4:
time: 74.2 us; the launch traced here: 74 us
  Pallas kernels  70.8 us (95%)
  local copies, waits for them, and re-layouts  3.17 us (4%)
    pallas_call x1, Pallas kernels, block_of(): pl.pallas_call(functools.partial(kernel, px, ny, nz), out_shape=jax.Shape...  70.8 us
    reshape x1, local copies, waits for them, and re-layouts, on_device(): new_hidden.reshape(batch * samples * steps, width)  1.76 us

profile of v4, /device:TPU:32, one launch (start us, length us, event | category | flops | bytes accessed | tf_op | source)
XLA Modules:
  0.0 74.0 jit_solution(3882507477487570164)
XLA Ops:
  0.0 1.8 %reshape.24.hid = bf16[32,5120]{1,0:T(8,128)(2,1)} reshape(bf16[4,2,4,5120]{3,2,1,0:T(4,128)(2,1)} %param.13) | data formatting | bytes 655360 | tf_op jit(solution)/shard_map/reshape | solution.py:570
  1.8 70.8 %block.1 = bf16[8,4,640]{2,1,0:T(4,128)(2,1)} custom-call(s32[4]{0:T(128)} %lengths.1, s32[2,4]{1,0:T(2,128)} %bitcast.15, bf16[32,5120]{1,0:T(8,128)(2,1)} %reshape.24.hid, bf16[160,1024]{1,0:T(8,128)(2,1)} %wq.1, bf16[160,128]{1,0:T(8,128)(2,1)} %wk.1, bf16[160,128]{1,0:T(8,128)(2,1)} %wv.1, bf16[160,1024]{1,0:T(8,128)(2,1)} %bitcast.13, ...), custom_call_target="tpu_custom_call" | custom-call | tf_op jit(solution)/shard_map/block/pallas_call | solution.py:527
  72.6 1.4 %copy.15 = bf16[4,2,4,640]{3,2,1,0:T(4,128)(2,1)} copy(bf16[4,2,4,640]{3,2,1,0:T(4,128)(2,1)} %bitcast.14) | data formatting | bytes 81920

commit v5 on v4

--- a/solution.py
+++ b/solution.py
@@ -180,6 +180,8 @@
                 else:
                     out.go(piece, spot, t_sem.at[0], device)
 
+    send_weights(1)
+
     def multiply(block, group):
         lhs = tok[block].reshape(2 * ny * rows, window)
         return jnp.dot(
@@ -189,11 +191,10 @@
     orow = pl.ds(pl.multiple_of(depth * c, 16), depth)
     orow_t = pl.ds(pl.multiple_of(depth * (1 - c), 16), depth)
 
-    def project(group, after):
+    def project(group):
         span = spans[group]
         arrived(wbuf.at[1, mine, span], w_sem.at[group])
         out.go(wbuf.at[1, mine, span], wbuf.at[1, mine, span], tw_sem.at[group, 1], twin)
-        after()
         arrived(wbuf.at[0, mine, span], loc.at[group])
         arrived(wbuf.at[0, theirs, span], tw_sem.at[group, 0])
         if group == 0:
@@ -291,7 +292,7 @@
         lw[1, pl.ds(b, 1), :] = lanes_of(lse[gr:], gr)
 
     half = batch // 2
-    project(0, lambda: send_weights(1))
+    project(0)
 
     def send_wo():
         for which in range(3):
@@ -299,7 +300,7 @@
         out.go(wo, obuf.at[x, orow], ot_sem.at[0], twin)
         pltpu.make_async_copy(wo, obuf.at[x, orow], loc.at[2]).start()
 
-    project(1, lambda: None)
+    project(1)
     own(0)
     total = own(1)
     send_wo()

time: 74.2 us -> 72.7 us (0.980)
  Pallas kernels: 70.8 us -> 69.3 us
    pallas_call x1, Pallas kernels: 70.8 us -> 69.3 us  [block_of(): pl.pallas_call(functools.partial(kernel, px, ny, nz), out_shape=jax.Shape...]
where the time goes in v5:
time: 72.7 us; the launch traced here: 72.5 us
  Pallas kernels  69.3 us (95%)
  local copies, waits for them, and re-layouts  3.17 us (4%)
    pallas_call x1, Pallas kernels, block_of(): pl.pallas_call(functools.partial(kernel, px, ny, nz), out_shape=jax.Shape...  69.3 us
    reshape x1, local copies, waits for them, and re-layouts, on_device(): new_hidden.reshape(batch * samples * steps, width)  1.76 us

profile of v5, /device:TPU:32, one launch (start us, length us, event | category | flops | bytes accessed | tf_op | source)
XLA Modules:
  0.0 72.5 jit_solution(3912718677756771946)
XLA Ops:
  0.0 1.8 %reshape.24.hid = bf16[32,5120]{1,0:T(8,128)(2,1)} reshape(bf16[4,2,4,5120]{3,2,1,0:T(4,128)(2,1)} %param.13) | data formatting | bytes 655360 | tf_op jit(solution)/shard_map/reshape | solution.py:571
  1.8 69.3 %block.1 = bf16[8,4,640]{2,1,0:T(4,128)(2,1)} custom-call(s32[4]{0:T(128)} %lengths.1, s32[2,4]{1,0:T(2,128)} %bitcast.15, bf16[32,5120]{1,0:T(8,128)(2,1)} %reshape.24.hid, bf16[160,1024]{1,0:T(8,128)(2,1)} %wq.1, bf16[160,128]{1,0:T(8,128)(2,1)} %wk.1, bf16[160,128]{1,0:T(8,128)(2,1)} %wv.1, bf16[160,1024]{1,0:T(8,128)(2,1)} %bitcast.13, ...), custom_call_target="tpu_custom_call" | custom-call | tf_op jit(solution)/shard_map/block/pallas_call | solution.py:528
  71.1 1.4 %copy.15 = bf16[4,2,4,640]{3,2,1,0:T(4,128)(2,1)} copy(bf16[4,2,4,640]{3,2,1,0:T(4,128)(2,1)} %bitcast.14) | data formatting | bytes 81920
